TPU v7x, 128 devices: a whole 4x4x4 slice. The times are simulated.
128 devices in a mesh: row: 16 (over y, x), col: 8 (over z, core).
Axes of the slice: x: 4, y: 4, z: 4, core: 2. Of those that a mesh axis runs over, the one named last changes fastest.
Arguments:
- object_field: float32 [2, 4096, 8192], P(None, 'row', 'col'), may hold values from -5 to 5
- probe_modes: float32 [4, 2, 256, 256], replicated, may hold values from -4 to 4
- offsets: int32 [2, 384, 2], P(None, ('row', 'col')), may hold values from 0 to 7936, as said below
- live_counts: int32 [2, 128], P(None, ('row', 'col')), may hold values from 1 to 3, as said below
- patterns: float32 [2, 384, 256, 256], P(None, ('row', 'col')), may hold values from 0 to 4
Outputs:
- new_object: float32 [2, 4096, 8192], P(None, 'row', 'col')
- new_probe: float32 [4, 2, 256, 256], replicated
Inputs may be any that keep to these rules, and one draw needn't show every extreme that they name: `offsets`: slots d * 3 to (d + 1) * 3 - 1 belong to device d (row-major over the mesh, d = row * 8 + col); each such slot's top-left pixel lies in that device's tile of 256 x 1024 pixels, and every window lies inside the object. Only the first live_counts[b, d] slots of device d are live in batch b; in every batch some device has exactly 3.
All inputs are finite; a program needn't handle non-finite values.
Results may differ from a plain program's by a relative error of at most 0.0003.
Values sent between devices are 32-bit elements; how exact they have to be, the bound alone decides.
A program may use at most 384 MiB of HBM per device.

v0:
```python
import math

import jax
import jax.numpy as jnp
from jax import lax
from jax.sharding import PartitionSpec as P

highest = lax.Precision.HIGHEST
step_object = 1.0
step_probe = 1.0
smoothing = 0.05
object_floor = 1.0
probe_floor = 0.001


def shifted(value, axis, steps):
    count = lax.axis_size(axis)
    leading, last = (max(0, -steps), min(count, count - steps))
    return lax.ppermute(value, axis, [(source, source + steps) for source in range(leading, last)])


def padded(shard, sides, width):
    for axis, dim in sides:
        count, length = (lax.axis_size(axis), shard.shape[dim])
        up = [(i, (i + 1) % count) for i in range(count - 1)]
        down = [(j, i) for i, j in up]
        last = lax.slice_in_dim(shard, length - width, length, axis=dim)
        leading = lax.slice_in_dim(shard, 0, width, axis=dim)
        before = lax.ppermute(last, axis, up)
        after = lax.ppermute(leading, axis, down)
        shard = jnp.concatenate([before, shard, after], axis=dim)
    return shard


def transform(real_part, imag_part, cos_table, sin_table):

    def apply_rows(matrix, values):
        return jnp.einsum("jk,mkl->mjl", matrix, values, precision=highest)

    def apply_columns(values, matrix):
        return jnp.einsum("mjk,kl->mjl", values, matrix, precision=highest)

    middle_real = apply_rows(cos_table, real_part) - apply_rows(sin_table, imag_part)
    middle_imag = apply_rows(cos_table, imag_part) + apply_rows(sin_table, real_part)
    outer_real = apply_columns(middle_real, cos_table) - apply_columns(middle_imag, sin_table)
    outer_imag = apply_columns(middle_imag, cos_table) + apply_columns(middle_real, sin_table)
    return (outer_real, outer_imag)


def process_item(window, pattern, probe_modes, cos_table, sin_table):
    probe_real = probe_modes[:, 0]
    probe_imag = probe_modes[:, 1]
    window_real = window[0]
    window_imag = window[1]
    wave_real = probe_real * window_real - probe_imag * window_imag
    wave_imag = probe_real * window_imag + probe_imag * window_real
    far_real, far_imag = transform(wave_real, wave_imag, cos_table, -sin_table)
    intensity = jnp.sum(far_real * far_real + far_imag * far_imag, axis=0)
    misfit = intensity - pattern
    back_real, back_imag = transform(misfit * far_real, misfit * far_imag, cos_table, sin_table)
    object_term = jnp.stack(
        [
            jnp.sum(probe_real * back_real + probe_imag * back_imag, axis=0),
            jnp.sum(probe_real * back_imag - probe_imag * back_real, axis=0),
        ]
    )
    probe_term = jnp.stack(
        [
            window_real * back_real + window_imag * back_imag,
            window_real * back_imag - window_imag * back_real,
        ],
        axis=1,
    )
    window_power = window_real * window_real + window_imag * window_imag
    return (object_term, probe_term, window_power)


def run_items(
    first_item,
    last_item,
    slot_of,
    window_set,
    pattern_set,
    probe_modes,
    cos_table,
    sin_table,
    slot_count,
):
    side_len = probe_modes.shape[-1]

    def visit_item(position, state_now):
        results, probe_total, power_total = state_now
        slot_at = slot_of(position)
        window = lax.dynamic_index_in_dim(window_set, slot_at, 0, keepdims=False)
        pattern = lax.dynamic_index_in_dim(pattern_set, slot_at, 0, keepdims=False)
        object_term, probe_term, window_power = process_item(
            window, pattern, probe_modes, cos_table, sin_table
        )
        results = lax.dynamic_update_index_in_dim(results, object_term, slot_at, 0)
        return (results, probe_total + probe_term, power_total + window_power)

    start_state = (
        jnp.zeros((slot_count, 2, side_len, side_len), jnp.float32),
        jnp.zeros(probe_modes.shape, jnp.float32),
        jnp.zeros((side_len, side_len), jnp.float32),
    )
    return lax.fori_loop(first_item, last_item, visit_item, start_state)


def one_batch(object_field, probe_modes, local_spots, own_count, pattern_set, cos_table, sin_table):
    side_len = probe_modes.shape[-1]
    tile_rows = object_field.shape[1]
    tile_cols = object_field.shape[2]
    capacity = local_spots.shape[0]
    right_rim = shifted(object_field[:, :, :side_len], "col", -1)
    widened = jnp.concatenate([object_field, right_rim], axis=2)
    lower_rim = shifted(widened, "row", -1)
    extended = jnp.concatenate([widened, lower_rim], axis=1)
    bordered = padded(object_field, (("row", 1), ("col", 2)), 1)

    def cut_window(location):
        return lax.dynamic_slice(
            extended, (jnp.int32(0), location[0], location[1]), (2, side_len, side_len)
        )

    window_set = jax.vmap(cut_window)(local_spots)

    def own_slot(position):
        return position

    item_grads, probe_total, power_total = run_items(
        jnp.int32(0),
        own_count,
        own_slot,
        window_set,
        pattern_set,
        probe_modes,
        cos_table,
        sin_table,
        capacity,
    )
    probe_power = jnp.sum(probe_modes * probe_modes, axis=(0, 1))

    def place_item(position, accum):
        location = lax.dynamic_index_in_dim(local_spots, position, 0, keepdims=False)
        contribution = jnp.concatenate(
            [lax.dynamic_index_in_dim(item_grads, position, 0, keepdims=False), probe_power[None]],
            axis=0,
        )
        start_at = (jnp.int32(0), location[0], location[1])
        current = lax.dynamic_slice(accum, start_at, (3, side_len, side_len))
        return lax.dynamic_update_slice(accum, current + contribution, start_at)

    accum = jnp.zeros((3, tile_rows + side_len, tile_cols + side_len), jnp.float32)
    accum = lax.fori_loop(jnp.int32(0), own_count, place_item, accum)
    from_above = shifted(accum[:, tile_rows:, :], "row", 1)
    banded = accum[:, :tile_rows, :].at[:, :side_len, :].add(from_above)
    from_left = shifted(banded[:, :, tile_cols:], "col", 1)
    gathered = banded[:, :, :tile_cols].at[:, :, :side_len].add(from_left)
    neighbours = (
        bordered[:, 2:, 1:-1]
        + bordered[:, :-2, 1:-1]
        + bordered[:, 1:-1, 2:]
        + bordered[:, 1:-1, :-2]
    )
    laplace_term = neighbours - 4.0 * object_field
    new_object = (
        object_field
        - step_object * gathered[:2] / (gathered[2] + object_floor)
        + step_object * smoothing * laplace_term
    )
    total_grad, total_power = lax.psum((probe_total, power_total), ("row", "col"))
    new_probe = probe_modes - step_probe * total_grad / (total_power + probe_floor)
    return (new_object, new_probe)


def shards(object_field, probe_modes, offsets, live_counts, patterns):
    side_len = probe_modes.shape[-1]
    tile_rows = object_field.shape[1]
    tile_cols = object_field.shape[2]
    indices = jnp.arange(side_len, dtype=jnp.int32)
    phases = (indices[:, None] * indices[None, :] % side_len).astype(jnp.float32) * (
        2.0 * math.pi / side_len
    )
    norm_scale = 1.0 / math.sqrt(side_len)
    cos_table = jnp.cos(phases) * norm_scale
    sin_table = jnp.sin(phases) * norm_scale
    anchor = jnp.stack([lax.axis_index("row") * tile_rows, lax.axis_index("col") * tile_cols])
    for batch_index in range(offsets.shape[0]):
        local_spots = offsets[batch_index] - anchor[None, :]
        object_field, probe_modes = one_batch(
            object_field,
            probe_modes,
            local_spots,
            live_counts[batch_index, 0],
            patterns[batch_index],
            cos_table,
            sin_table,
        )
    return (object_field, probe_modes)


def solution(mesh):
    placed = (
        P(None, "row", "col"),
        P(),
        P(None, ("row", "col"), None),
        P(None, ("row", "col")),
        P(None, ("row", "col"), None, None),
    )
    return jax.shard_map(
        shards, mesh=mesh, in_specs=placed, out_specs=(P(None, "row", "col"), P()), check_vma=False
    )
```

profile of v0, /device:TPU:1, one launch (start us, length us, event | category | flops | bytes accessed | tf_op | source)
XLA Modules:
  0.0 1079.7 jit_solution(11788223931382341118)
XLA Ops:
  14.8 5.6 collective-permute-done
  27.1 49.3 %collective-permute-done.1 = f32[2,256,1280]{2,1,0:T(8,128)} collective-permute-done((f32[2,256,1280]{2,1,0:T(8,128)}, f32[2,256,1280]{2,1,0:T(8,128)}, u32[]{:S(2)}, u32[]{:S(2)}) %collective-permute-start.1) | collective-permute-done | bytes 2621472 | tf_op jit(solution)/shard_map/ppermute | solution.py:19
  76.4 5.2 pad_maximum_fusion
  82.8 12.1 %while.64 = (s32[]{:T(128)}, f32[2,512,1280]{2,1,0:T(8,128)}, s32[3,3]{1,0:T(4,128)S(1)}, f32[3,2,256,256]{3,2,1,0:T(8,128)}, s32[]{:T(128)}) while((s32[]{:T(128)}, f32[2,512,1280]{2,1,0:T(8,128)}, s32[3,3]{1,0:T(4,128)S(1)}, f32[3,2,256,256]{3,2,1,0:T(8,128)}, s32[]{:T(128)}) %tuple.181), condition=%wide.while_cond.4, body=%wide.while_body.4.sunk | while | flops 2 | bytes 1050217 | solution.py:122
  83.4 3.4 bitcast_dynamic-update-slice_fusion.4
  97.8 58.7 %while.66 = (s32[]{:T(128)}, f32[3,2,256,256]{3,2,1,0:T(8,128)}, f32[4,2,256,256]{3,2,0,1:T(8,128)}, f32[256,256]{1,0:T(8,128)S(1)}, s32[]{:T(128)}, /*index=5*/...) while((s32[]{:T(128)}, f32[3,2,256,256]{3,2,1,0:T(8,128)}, ...), condition=%wide.region_4.5_spmd.clone.clone, body=%wide.region_0.4_spmd.clone.clone.sunk | while | flops 12913213440 | bytes 82313456 | solution.py:107
  159.7 259.9 %all-reduce.7.cloned.1.call-done = (f32[4,2,256,256]{3,2,1,0:T(8,128)}, f32[256,256]{1,0:T(8,128)}) async-done(((f32[4,2,256,256]{3,2,1,0:T(8,128)}, f32[256,256]{1,0:T(8,128)}), (f32[4,2,256,256]{3,2,1,0:T(8,128)}, f32[256,256]{1,0:T(8,128)})) %all-reduce.7.cloned.1.call-update) | async-done | bytes 2359312 | tf_op jit(solution)/shard_map/psum | solution.py:172
  420.5 4.0 multiply_reduce_fusion
  424.5 3.7 broadcast.164.clone
  428.2 17.6 %while.62 = (s32[]{:T(128)}, f32[3,512,1280]{2,1,0:T(8,128)}, s32[]{:T(128)}, s32[3,2]{0,1:T(2,128)S(1)}, f32[3,2,256,256]{3,2,1,0:T(8,128)}, /*index=5*/f32[256...) while((s32[]{:T(128)}, f32[3,512,1280]{2,1,0:T(8,128)}, s32[]{:T(128)}, ...), condition=%wide.region_7.8_spmd, body=%wide.region_6.7_spmd.sunk | while | flops 393227 | bytes 4980999 | solution.py:155
  436.3 8.8 dynamic_update_slice.25
  448.3 36.2 %collective-permute-start.2 = (f32[3,256,1280]{2,1,0:T(8,128)S(1)}, f32[3,256,1280]{2,1,0:T(8,128)S(1)}, u32[]{:S(2)}, u32[]{:S(2)}) collective-permute-start(f32[3,256,1280]{2,1,0:T(8,128)S(1)} %slice.275), channel_id=1, source_target_pairs={{0,8},{8,16},{16,24},{24,32},{32,40},{40,48},{48,56},{56,64},{64,7... | collective-permute-start | bytes 11796488 | tf_op jit(solution)/shard_map/ppermute | solution.py:19
  484.5 53.5 %collective-permute-done.2 = f32[3,256,1280]{2,1,0:T(8,128)S(1)} collective-permute-done((f32[3,256,1280]{2,1,0:T(8,128)S(1)}, f32[3,256,1280]{2,1,0:T(8,128)S(1)}, u32[]{:S(2)}, u32[]{:S(2)}) %collective-permute-start.2) | collective-permute-done | bytes 3932192 | tf_op jit(solution)/shard_map/ppermute | solution.py:19
  541.8 4.4 collective-permute-start.5
  561.4 9.7 collective-permute-done.8
  576.1 50.1 %collective-permute-done.9 = f32[2,256,1280]{2,1,0:T(8,128)} collective-permute-done((f32[2,256,1280]{2,1,0:T(8,128)}, f32[2,256,1280]{2,1,0:T(8,128)}, u32[]{:S(2)}, u32[]{:S(2)}) %collective-permute-start.9) | collective-permute-done | bytes 2621472 | tf_op jit(solution)/shard_map/ppermute | solution.py:19
  626.2 4.5 pad_maximum_fusion.1
  632.0 12.2 %while.65 = (s32[]{:T(128)}, f32[2,512,1280]{2,1,0:T(8,128)}, s32[3,3]{1,0:T(4,128)S(1)}, f32[3,2,256,256]{3,2,1,0:T(8,128)}, s32[]{:T(128)}) while((s32[]{:T(128)}, f32[2,512,1280]{2,1,0:T(8,128)}, s32[3,3]{1,0:T(4,128)S(1)}, f32[3,2,256,256]{3,2,1,0:T(8,128)}, s32[]{:T(128)}) %tuple.190), condition=%wide.while_cond.5, body=%wide.while_body.5.sunk | while | flops 2 | bytes 1050217 | solution.py:122
  647.1 55.8 %while.67 = (s32[]{:T(128)}, f32[3,2,256,256]{3,2,1,0:T(8,128)}, f32[4,2,256,256]{3,2,0,1:T(8,128)}, f32[256,256]{1,0:T(8,128)S(1)}, s32[]{:T(128)}, /*index=5*/...) while((s32[]{:T(128)}, f32[3,2,256,256]{3,2,1,0:T(8,128)}, ...), condition=%wide.region_14.15_spmd.clone.clone, body=%wide.region_10.14_spmd.clone.clone.sunk | while | flops 12913213440 | bytes 82313456 | solution.py:107
  702.9 3.7 broadcast.164
  706.6 17.0 %while.63 = (s32[]{:T(128)}, f32[3,512,1280]{2,1,0:T(8,128)}, s32[]{:T(128)}, s32[3,2]{0,1:T(2,128)S(1)}, f32[3,2,256,256]{3,2,1,0:T(8,128)}, /*index=5*/f32[256...) while((s32[]{:T(128)}, f32[3,512,1280]{2,1,0:T(8,128)}, ...), condition=%wide.region_17.18_spmd, body=%wide.region_16.17_spmd.sunk | while | flops 393227 | bytes 4980999 | solution.py:155
  714.1 8.8 dynamic_update_slice.26
  723.6 4.4 slice.296
  728.0 36.1 %collective-permute-start.10 = (f32[3,256,1280]{2,1,0:T(8,128)}, f32[3,256,1280]{2,1,0:T(8,128)}, u32[]{:S(2)}, u32[]{:S(2)}) collective-permute-start(f32[3,256,1280]{2,1,0:T(8,128)} %slice.296), channel_id=1, source_target_pairs={{0,8},{8,16},{16,24},{24,32},{32,40},{40,48},{48,56},{56,64},{64,7... | collective-permute-start | bytes 11796488 | tf_op jit(solution)/shard_map/ppermute | solution.py:19
  765.6 39.5 %collective-permute-done.10 = f32[3,256,1280]{2,1,0:T(8,128)} collective-permute-done((f32[3,256,1280]{2,1,0:T(8,128)}, f32[3,256,1280]{2,1,0:T(8,128)}, u32[]{:S(2)}, u32[]{:S(2)}) %collective-permute-start.10) | collective-permute-done | bytes 3932192 | tf_op jit(solution)/shard_map/ppermute | solution.py:19
  805.2 3.8 slice_add_fusion
  809.0 156.3 %collective-permute-start.11 = (f32[3,256,256]{2,1,0:T(8,128)S(1)}, f32[3,256,256]{2,1,0:T(8,128)}, u32[]{:S(2)}, u32[]{:S(2)}) collective-permute-start(f32[3,256,256]{2,1,0:T(8,128)S(1)} %slice.364), channel_id=1, source_target_pairs={{0,1},{1,2},{2,3},{3,4},{4,5},{5,6},{6,7},{8,9},{9,10},{10,11},{11... | collective-permute-start | bytes 2359304 | tf_op jit(solution)/shard_map/ppermute | solution.py:19
  966.7 4.8 collective-permute-start.13
  975.1 3.6 collective-permute-start.15
  978.7 81.5 %all-reduce.5.cloned.1.call-done = (f32[4,2,256,256]{3,2,1,0:T(8,128)}, f32[256,256]{1,0:T(8,128)}) async-done(((f32[4,2,256,256]{3,2,1,0:T(8,128)}, f32[256,256]{1,0:T(8,128)}), (f32[4,2,256,256]{3,2,1,0:T(8,128)}, f32[256,256]{1,0:T(8,128)})) %all-reduce.5.cloned.1.call-update) | async-done | bytes 2359312 | tf_op jit(solution)/shard_map/psum | solution.py:172
  1061.2 4.0 divide_subtract_fusion
  1068.5 4.2 fusion.291
  (175 shorter events, 189.6 us)
Async XLA Ops:
  7.2 412.4 %all-reduce.7.cloned.1.call-start = ((), (), s32[]{:S(2)}) async-start(), calls=%async_computation.1 | async-start | bytes 4718592 | tf_op jit(solution)/shard_map/psum | solution.py:172
  8.3 14.5 %copy-start.19 = (s32[2,3,2]{1,2,0:T(2,128)S(1)}, s32[2,3,2]{1,2,0:T(2,128)}, u32[]{:S(2)}) copy-start(s32[2,3,2]{1,2,0:T(2,128)} %param.27) | copy-start | bytes 148
  8.3 12.2 %collective-permute-start = (f32[2,256,256]{2,1,0:T(8,128)S(1)}, f32[2,256,256]{2,1,0:T(8,128)S(1)}, u32[]{:S(2)}, u32[]{:S(2)}) collective-permute-start(f32[2,256,256]{2,1,0:T(8,128)S(1)} %slice.270), channel_id=1, source_target_pairs={{1,0},{2,1},{3,2},{4,3},{5,4},{6,5},{7,6},{9,8},{10,9},{11,10},{12... | collective-permute-start | bytes 1572872 | tf_op jit(solution)/shard_map/ppermute | solution.py:19
  21.4 55.0 %collective-permute-start.1 = (f32[2,256,1280]{2,1,0:T(8,128)}, f32[2,256,1280]{2,1,0:T(8,128)}, u32[]{:S(2)}, u32[]{:S(2)}) collective-permute-start(f32[2,256,1280]{2,1,0:T(8,128)} %constant_dynamic-update-slice_fusion), channel_id=1, source_target_pairs={{8,0},{16,8},{24,16},{32,24},{40,32},{48,40},{56,48},{64,56},{72,6... | collective-permute-start | bytes 7864328 | tf_op jit(solution)/shard_map/ppermute | solution.py:19
  142.7 3.3 copy-start
  159.6 900.6 %all-reduce.5.cloned.1.call-start = ((), (), s32[]{:S(2)}) async-start(), calls=%async_computation | async-start | bytes 4718592 | tf_op jit(solution)/shard_map/psum | solution.py:172
  445.8 92.2 %copy-start.8 = (f32[3,512,1280]{2,1,0:T(8,128)S(1)}, f32[3,512,1280]{2,1,0:T(8,128)}, u32[]{:S(2)}) copy-start(f32[3,512,1280]{2,1,0:T(8,128)} %get-tuple-element.413) | copy-start | bytes 23592964
  448.3 92.1 %copy-start.9 = (f32[2,256,1024]{2,1,0:T(8,128)S(1)}, f32[2,256,1024]{2,1,0:T(8,128)}, u32[]{:S(2)}) copy-start(f32[2,256,1024]{2,1,0:T(8,128)} %param.25) | copy-start | bytes 6291460
  448.3 89.7 %collective-permute-start.2 = (f32[3,256,1280]{2,1,0:T(8,128)S(1)}, f32[3,256,1280]{2,1,0:T(8,128)S(1)}, u32[]{:S(2)}, u32[]{:S(2)}) collective-permute-start(f32[3,256,1280]{2,1,0:T(8,128)S(1)} %slice.275), channel_id=1, source_target_pairs={{0,8},{8,16},{16,24},{24,32},{32,40},{40,48},{48,56},{56,64},{64,7... | collective-permute-start | bytes 11796488 | tf_op jit(solution)/shard_map/ppermute | solution.py:19
  538.5 14.7 %collective-permute-start.3 = (f32[3,256,256]{2,1,0:T(8,128)S(1)}, f32[3,256,256]{2,1,0:T(8,128)S(1)}, u32[]{:S(2)}, u32[]{:S(2)}) collective-permute-start(f32[3,256,256]{2,1,0:T(8,128)S(1)} %slice.358), channel_id=1, source_target_pairs={{0,1},{1,2},{2,3},{3,4},{4,5},{5,6},{6,7},{8,9},{9,10},{10,11},{11... | collective-permute-start | bytes 2359304 | tf_op jit(solution)/shard_map/ppermute | solution.py:19
  540.5 5.7 collective-permute-start.4
  541.8 5.2 collective-permute-start.5
  547.2 7.8 collective-permute-start.6
  550.5 5.6 collective-permute-start.7
  559.4 13.4 %copy-start.5 = (f32[2,256,1024]{2,1,0:T(8,128)}, f32[2,256,1024]{2,1,0:T(8,128)S(1)}, u32[]{:S(2)}) copy-start(f32[2,256,1024]{2,1,0:T(8,128)S(1)} %fusion.298) | copy-start | bytes 6291460
  559.4 11.6 %collective-permute-start.8 = (f32[2,256,256]{2,1,0:T(8,128)S(1)}, f32[2,256,256]{2,1,0:T(8,128)S(1)}, u32[]{:S(2)}, u32[]{:S(2)}) collective-permute-start(f32[2,256,256]{2,1,0:T(8,128)S(1)} %slice.361), channel_id=1, source_target_pairs={{1,0},{2,1},{3,2},{4,3},{5,4},{6,5},{7,6},{9,8},{10,9},{11,10},{12... | collective-permute-start | bytes 1572872 | tf_op jit(solution)/shard_map/ppermute | solution.py:19
  572.8 53.4 %collective-permute-start.9 = (f32[2,256,1280]{2,1,0:T(8,128)}, f32[2,256,1280]{2,1,0:T(8,128)}, u32[]{:S(2)}, u32[]{:S(2)}) collective-permute-start(f32[2,256,1280]{2,1,0:T(8,128)} %pad_maximum_fusion.2), channel_id=1, source_target_pairs={{8,0},{16,8},{24,16},{32,24},{40,32},{48,40},{56,48},{64,56},{72,6... | collective-permute-start | bytes 7864328 | tf_op jit(solution)/shard_map/ppermute | solution.py:19
  574.1 52.0 %copy-start.6 = (f32[2,256,1024]{2,1,0:T(8,128)S(1)}, f32[2,256,1024]{2,1,0:T(8,128)}, u32[]{:S(2)}) copy-start(f32[2,256,1024]{2,1,0:T(8,128)} %copy-done.5) | copy-start | bytes 6291460
  574.1 52.0 %copy-start.15 = (f32[2,256,256]{2,1,0:T(8,128)S(1)}, f32[2,256,256]{2,1,0:T(8,128)}, u32[]{:S(2)}) copy-start(f32[2,256,256]{2,1,0:T(8,128)} %copy-done.14) | copy-start | bytes 1572868
  690.8 3.3 copy-start.2
  702.9 3.7 copy-start.13
  702.9 3.7 copy-start.18
  723.6 40.5 %copy-start.4 = (f32[4,2,256,256]{3,2,0,1:T(8,128)S(1)}, f32[4,2,256,256]{3,2,0,1:T(8,128)}, u32[]{:S(2)}) copy-start(f32[4,2,256,256]{3,2,0,1:T(8,128)} %get-tuple-element.418) | copy-start | bytes 6291460
  728.0 77.1 %collective-permute-start.10 = (f32[3,256,1280]{2,1,0:T(8,128)}, f32[3,256,1280]{2,1,0:T(8,128)}, u32[]{:S(2)}, u32[]{:S(2)}) collective-permute-start(f32[3,256,1280]{2,1,0:T(8,128)} %slice.296), channel_id=1, source_target_pairs={{0,8},{8,16},{16,24},{24,32},{32,40},{40,48},{48,56},{56,64},{64,7... | collective-permute-start | bytes 11796488 | tf_op jit(solution)/shard_map/ppermute | solution.py:19
  765.6 199.8 %copy-start.7 = (f32[2,256,1024]{2,1,0:T(8,128)S(1)}, f32[2,256,1024]{2,1,0:T(8,128)}, u32[]{:S(2)}) copy-start(f32[2,256,1024]{2,1,0:T(8,128)} %copy-done.5) | copy-start | bytes 6291460
  808.9 164.2 %copy-start.10 = (f32[3,256,1280]{2,1,0:T(8,128)}, f32[3,256,1280]{2,1,0:T(8,128)S(1)}, u32[]{:S(2)}) copy-start(f32[3,256,1280]{2,1,0:T(8,128)S(1)} %slice_add_fusion) | copy-start | bytes 11796484
  809.0 256.2 %collective-permute-start.11 = (f32[3,256,256]{2,1,0:T(8,128)S(1)}, f32[3,256,256]{2,1,0:T(8,128)}, u32[]{:S(2)}, u32[]{:S(2)}) collective-permute-start(f32[3,256,256]{2,1,0:T(8,128)S(1)} %slice.364), channel_id=1, source_target_pairs={{0,1},{1,2},{2,3},{3,4},{4,5},{5,6},{6,7},{8,9},{9,10},{10,11},{11... | collective-permute-start | bytes 2359304 | tf_op jit(solution)/shard_map/ppermute | solution.py:19
  965.4 6.1 collective-permute-start.12
  966.7 5.5 collective-permute-start.13
  973.1 95.3 %collective-permute-start.14 = (f32[2,258,1]{2,1,0:T(8,128)}, f32[2,258,1]{2,1,0:T(8,128)S(1)}, u32[]{:S(2)}, u32[]{:S(2)}) collective-permute-start(f32[2,258,1]{2,1,0:T(8,128)} %get-tuple-element.696), channel_id=1, source_target_pairs={{1,0},{2,1},{3,2},{4,3},{5,4},{6,5},{7,6},{9,8},{10,9},{11,10},{12... | collective-permute-start | bytes 6200 | tf_op jit(solution)/shard_map/ppermute | solution.py:30
  975.1 93.4 %collective-permute-start.15 = (f32[2,258,1]{2,1,0:T(8,128)}, f32[2,258,1]{2,1,0:T(8,128)S(1)}, u32[]{:S(2)}, u32[]{:S(2)}) collective-permute-start(f32[2,258,1]{2,1,0:T(8,128)} %get-tuple-element.697), channel_id=1, source_target_pairs={{0,1},{1,2},{2,3},{3,4},{4,5},{5,6},{6,7},{8,9},{9,10},{10,11},{11... | collective-permute-start | bytes 6200 | tf_op jit(solution)/shard_map/ppermute | solution.py:29
  1061.2 4.0 copy-start.11
  (8 other events, 14.5 us)
Sparse Core Ops, SparseCore 0:
  159.7 259.7 all-reduce.6
  765.7 294.4 all-reduce.4
where the time goes:
time: 1090 us; the launch traced here: 1080 us
  waiting for transfers between devices  553 us (51%)
  starting transfers between devices  261 us (24%)
  matrix products  89.7 us (8%)
  local copies, waits for them, and re-layouts  89.3 us (8%)
  other arithmetic  45.1 us (4%)
  loops' own time  26.4 us (2%)
  between operations  14.7 us (1%)
    psum x2, waiting for transfers between devices, one_batch(): lax.psum((probe_total, power_total), ('row', 'col'))  341 us
    ppermute x8, starting transfers between devices, shifted(): lax.ppermute(value, axis, [(source, source + steps) for source in range(l...  238 us
    ppermute x8, waiting for transfers between devices, shifted(): lax.ppermute(value, axis, [(source, source + steps) for source in range(l...  208 us
    dot_general x16, matrix products, apply_columns(): return jnp.einsum('mjk,kl->mjl', values, matrix, precision=highest)  45.9 us
    dot_general x16, matrix products, apply_rows(): return jnp.einsum('jk,mkl->mjl', matrix, values, precision=highest)  43.8 us
    gather x18, local copies, waits for them, and re-layouts  24.3 us
  transfers between devices with their start and end apart: 18, of which 12 were waited for; matrix products, arithmetic and copies ran while one was open for 2% of the time, Pallas kernels for 0%

commit v1 on v0

v1 whole, which is shorter than its diff:
```python
import math

import jax
import jax.numpy as jnp
import ml_dtypes
import numpy as np
from jax import lax
from jax.experimental import pallas as pl
from jax.experimental.pallas import tpu as pltpu
from jax.sharding import PartitionSpec as P

step_object = 1.0
step_probe = 1.0
smoothing = 0.05
object_floor = 1.0
probe_floor = 0.001
SIDE = 256
HALF = 128
MODES = 4
VMEM = pltpu.VMEM
f32 = jnp.float32


def shifted(value, axis, steps):
    count = lax.axis_size(axis)
    leading, last = (max(0, -steps), min(count, count - steps))
    return lax.ppermute(value, axis, [(source, source + steps) for source in range(leading, last)])


def matrices():
    k, n = np.arange(HALF)[:, None], np.arange(HALF)[None, :]
    out = []
    for odd in (0, 1):
        angle = -2.0 * np.pi * (((2 * k + odd) * n) % SIDE) / SIDE
        re, im = np.cos(angle) / math.sqrt(SIDE), np.sin(angle) / math.sqrt(SIDE)
        big = np.block([[re, -im], [im, re]])
        for matrix in (big, big.T):
            high = matrix.astype(ml_dtypes.bfloat16)
            low = (matrix - high.astype(np.float64)).astype(ml_dtypes.bfloat16)
            out += [high, low]
    return np.stack(out)


def split(value):
    high = value.astype(jnp.bfloat16)
    return high, (value - high.astype(f32)).astype(jnp.bfloat16)


def dot(a, b):
    return jnp.dot(a, b, preferred_element_type=f32)


def left(mats, index, value):
    high, low = split(value)
    a, b = mats[index], mats[index + 1]
    return dot(a, high) + dot(b, high) + dot(a, low)


def right(value, mats, index):
    high, low = split(value)
    a, b = mats[index], mats[index + 1]
    return dot(high, a) + dot(high, b) + dot(low, a)


def cat(axis, *values):
    return jnp.concatenate(values, axis=axis)


def iotas():
    shape = (SIDE, SIDE)
    return lax.broadcasted_iota(jnp.int32, shape, 0), lax.broadcasted_iota(jnp.int32, shape, 1)


def roll2(value, rows, cols):
    return pltpu.roll(pltpu.roll(value, rows, 0), cols, 1)


def pattern_kernel(pat_ref, perm_ref, out_ref):
    high, low = split(pat_ref[0])
    value = dot(perm_ref[0], high) + dot(perm_ref[0], low)
    high, low = split(value)
    out_ref[0] = dot(high, perm_ref[1]) + dot(low, perm_ref[1])


def order_patterns(patterns):
    perm = np.zeros((SIDE, SIDE), np.float32)
    j = np.arange(SIDE)
    perm[j, (j % 2) * HALF + j // 2] = 1.0
    count = patterns.shape[0]
    block = pl.BlockSpec((1, SIDE, SIDE), lambda i: (i, 0, 0))
    return pl.pallas_call(
        pattern_kernel,
        grid=(count,),
        in_specs=[block, pl.BlockSpec((2, SIDE, SIDE), lambda i: (0, 0, 0))],
        out_specs=block,
        out_shape=jax.ShapeDtypeStruct(patterns.shape, f32),
        name="order_patterns",
    )(patterns, jnp.asarray(np.stack([perm.T, perm]), jnp.bfloat16))


def pack_kernel(last, sc, a_ref, b_ref, rim_ref, out_ref):
    _, cols = iotas()
    cm = sc[2]
    for part in range(2):
        after = jnp.where(sc[0] == last, rim_ref[part], b_ref[part])
        out_ref[part] = jnp.where(cols >= cm, a_ref[part], after)


def tile_specs(last):
    part = lambda index: pl.BlockSpec((2, SIDE, SIDE), index)
    return [
        part(lambda i, sc: (0, 0, sc[0])),
        part(lambda i, sc: (0, 0, jnp.minimum(sc[0] + 1, last))),
        part(lambda i, sc: (0, 0, 0)),
    ]


def pack(info, tile, rim):
    last = tile.shape[2] // SIDE - 1
    return pl.pallas_call(
        lambda *refs: pack_kernel(last, *refs),
        grid_spec=pltpu.PrefetchScalarGridSpec(
            num_scalar_prefetch=1,
            grid=(1,),
            in_specs=tile_specs(last),
            out_specs=pl.BlockSpec((2, SIDE, SIDE), lambda i, sc: (0, 0, 0)),
        ),
        out_shape=jax.ShapeDtypeStruct((2, SIDE, SIDE), f32),
        name="pack",
    )(info, tile, tile, rim)


def slot_kernel(last, first, sc, a_ref, b_ref, rim_ref, below_ref, pat_ref, probe_ref, mats, *refs):
    if first:
        w_ref, pg_ref, psi = refs
    else:
        pg_in, w_ref, pg_ref, psi = refs
    r, cm, live = sc[1], sc[2], sc[3]

    @pl.when(live == 0)
    def _():
        w_ref[...] = jnp.zeros_like(w_ref)
        if first:
            pg_ref[...] = jnp.zeros_like(pg_ref)
        else:
            pg_ref[...] = pg_in[...]

    @pl.when(live == 1)
    def _():
        rows, cols = iotas()
        window = []
        for part in range(2):
            after = jnp.where(sc[0] == last, rim_ref[part], b_ref[part])
            own = jnp.where(cols >= cm, a_ref[part], after)
            whole = jnp.where(rows >= r, own, below_ref[part])
            window.append(roll2(whole, lax.rem(SIDE - r, SIDE), lax.rem(SIDE - cm, SIDE)))
        xr, xi = window
        total_e = total_o = None
        for m in range(MODES):
            pr, pi = probe_ref[m, 0], probe_ref[m, 1]
            wr, wi = pr * xr - pi * xi, pr * xi + pi * xr
            even = left(mats, 0, cat(0, wr[:HALF] + wr[HALF:], wi[:HALF] + wi[HALF:]))
            odd = left(mats, 4, cat(0, wr[:HALF] - wr[HALF:], wi[:HALF] - wi[HALF:]))
            tr, ti = cat(0, even[:HALF], odd[:HALF]), cat(0, even[HALF:], odd[HALF:])
            pe = right(cat(1, tr[:, :HALF] + tr[:, HALF:], ti[:, :HALF] + ti[:, HALF:]), mats, 2)
            po = right(cat(1, tr[:, :HALF] - tr[:, HALF:], ti[:, :HALF] - ti[:, HALF:]), mats, 6)
            psi[m, 0], psi[m, 1] = pe, po
            total_e = pe * pe if m == 0 else total_e + pe * pe
            total_o = po * po if m == 0 else total_o + po * po
        de = total_e[:, :HALF] + total_e[:, HALF:] - pat_ref[0, :, :HALF]
        do = total_o[:, :HALF] + total_o[:, HALF:] - pat_ref[0, :, HALF:]
        de, do = cat(1, de, de), cat(1, do, do)
        grad_r = grad_i = None
        for m in range(MODES):
            ue, uo = right(psi[m, 0] * de, mats, 0), right(psi[m, 1] * do, mats, 4)
            plus, minus = ue + uo, ue - uo
            tr, ti = cat(1, plus[:, :HALF], minus[:, :HALF]), cat(1, plus[:, HALF:], minus[:, HALF:])
            ze = left(mats, 2, cat(0, tr[:HALF], ti[:HALF]))
            zo = left(mats, 6, cat(0, tr[HALF:], ti[HALF:]))
            plus, minus = ze + zo, ze - zo
            br, bi = cat(0, plus[:HALF], minus[:HALF]), cat(0, plus[HALF:], minus[HALF:])
            pr, pi = probe_ref[m, 0], probe_ref[m, 1]
            gr, gi = pr * br + pi * bi, pr * bi - pi * br
            grad_r = gr if m == 0 else grad_r + gr
            grad_i = gi if m == 0 else grad_i + gi
            tr, ti = xr * br + xi * bi, xr * bi - xi * br
            pg_ref[2 * m] = tr if first else pg_in[2 * m] + tr
            pg_ref[2 * m + 1] = ti if first else pg_in[2 * m + 1] + ti
        power = xr * xr + xi * xi
        pg_ref[2 * MODES] = power if first else pg_in[2 * MODES] + power
        w_ref[0] = roll2(grad_r, r, cm)
        w_ref[1] = roll2(grad_i, r, cm)


def run_slot(info, slot, tile, rim, below, patterns, probe, mats, pg):
    last = tile.shape[2] // SIDE - 1
    first = pg is None
    whole = lambda shape: pl.BlockSpec(shape, lambda i, sc: (0,) * len(shape))
    pg_shape = (2 * MODES + 1, SIDE, SIDE)
    return pl.pallas_call(
        lambda *refs: slot_kernel(last, first, *refs),
        grid_spec=pltpu.PrefetchScalarGridSpec(
            num_scalar_prefetch=1,
            grid=(1,),
            in_specs=tile_specs(last)
            + [
                whole((2, SIDE, SIDE)),
                pl.BlockSpec((1, SIDE, SIDE), lambda i, sc: (slot, 0, 0)),
                whole(probe.shape),
                whole(mats.shape),
            ]
            + ([] if first else [whole(pg_shape)]),
            out_specs=[whole((2, SIDE, SIDE)), whole(pg_shape)],
            scratch_shapes=[pltpu.VMEM((MODES, 2, SIDE, SIDE), f32)],
        ),
        out_shape=[
            jax.ShapeDtypeStruct((2, SIDE, SIDE), f32),
            jax.ShapeDtypeStruct(pg_shape, f32),
        ],
        compiler_params=pltpu.CompilerParams(vmem_limit_bytes=40 * 2**20),
        cost_estimate=pl.CostEstimate(flops=2 * 96 * SIDE**3, bytes_accessed=8 * 2**20, transcendentals=0),
        name="slot",
    )(info, tile, tile, rim, below, patterns, probe, mats, *([] if first else [pg]))


def prepare_kernel(sc, tile, above, below, before, rim, probe_ref, base_ref, weight_ref):
    chunks = weight_ref.shape[0]
    rows, cols = iotas()
    power = probe_ref[0, 0] * probe_ref[0, 0]
    for m in range(MODES):
        for part in range(2):
            if m or part:
                power = power + probe_ref[m, part] * probe_ref[m, part]
    weight_ref[...] = jnp.zeros_like(weight_ref)
    count = sc.shape[1]
    for where in range(4):
        for slot in range(count):
            k, r, cm, live = [sc[where, slot, j] for j in range(4)]
            is_left = where >= 2

            @pl.when((live == 1) & ((k == chunks - 1) if is_left else True))
            def _():
                value = roll2(power, r, cm)
                inside = (rows >= r) if where % 2 == 0 else (rows < r)
                value = jnp.where(inside, value, 0.0)
                if is_left:
                    weight_ref[0] += jnp.where(cols < cm, value, 0.0)
                else:
                    weight_ref[k] += jnp.where(cols >= cm, value, 0.0)

                    @pl.when(k < chunks - 1)
                    def _():
                        weight_ref[k + 1] += jnp.where(cols < cm, value, 0.0)

    height, width = tile.shape[1:]
    row_at = lax.broadcasted_iota(jnp.int32, (height, width), 0)
    col_at = lax.broadcasted_iota(jnp.int32, (height, width), 1)
    for part in range(2):
        here = tile[part]
        up = jnp.where(row_at == 0, above[part, 7:8, :], pltpu.roll(here, 1, 0))
        down = jnp.where(row_at == height - 1, below[part, 0:1, :], pltpu.roll(here, height - 1, 0))
        lhs = jnp.where(col_at == 0, before[part, :, HALF - 1 : HALF], pltpu.roll(here, 1, 1))
        rhs = jnp.where(col_at == width - 1, rim[part, :, 0:1], pltpu.roll(here, width - 1, 1))
        neighbours = up + down + lhs + rhs
        base_ref[part] = here + (step_object * smoothing) * (neighbours - 4.0 * here)


def prepare(infos, tile, rim, probe):
    above = shifted(tile[:, -8:, :], "row", 1)
    below = shifted(tile[:, :8, :], "row", -1)
    before = shifted(tile[:, :, -HALF:], "col", 1)
    chunks = tile.shape[2] // SIDE
    vmem = pl.BlockSpec(memory_space=VMEM)
    return pl.pallas_call(
        prepare_kernel,
        in_specs=[pl.BlockSpec(memory_space=pltpu.SMEM)] + [vmem] * 6,
        out_specs=[vmem, vmem],
        out_shape=[
            jax.ShapeDtypeStruct(tile.shape, f32),
            jax.ShapeDtypeStruct((chunks, SIDE, SIDE), f32),
        ],
        compiler_params=pltpu.CompilerParams(vmem_limit_bytes=40 * 2**20),
        cost_estimate=pl.CostEstimate(flops=2**25, bytes_accessed=8 * 2**20, transcendentals=0),
        name="prepare",
    )(infos, tile, above, below, before, rim, probe)


def gather_kernel(sc, *refs):
    acc = refs[-1]
    acc[...] = jnp.zeros_like(acc)
    rows, cols = iotas()
    count = sc.shape[1]
    for where in range(2):
        for slot in range(count):
            k, r, cm, live = [sc[where, slot, j] for j in range(4)]
            ref = refs[where * count + slot]

            @pl.when(live == 1)
            def _():
                inside = (rows >= r) if where == 0 else (rows < r)
                for part in range(2):
                    value = jnp.where(inside, ref[part], 0.0)
                    acc[k, part] += jnp.where(cols >= cm, value, 0.0)
                    acc[k + 1, part] += jnp.where(cols < cm, value, 0.0)


def gather(infos, own, arrived, chunks):
    vmem = pl.BlockSpec(memory_space=VMEM)
    return pl.pallas_call(
        gather_kernel,
        in_specs=[pl.BlockSpec(memory_space=pltpu.SMEM)] + [vmem] * (len(own) + len(arrived)),
        out_specs=vmem,
        out_shape=jax.ShapeDtypeStruct((chunks + 1, 2, SIDE, SIDE), f32),
        compiler_params=pltpu.CompilerParams(vmem_limit_bytes=40 * 2**20),
        name="gather",
    )(infos, *own, *arrived)


def update_kernel(base, acc, weight, extra, out):
    scale = step_object / (weight[0] + object_floor)

    @pl.when(pl.program_id(0) == 0)
    def _():
        for part in range(2):
            out[part] = base[part] - scale * (acc[0, part] + extra[part])

    @pl.when(pl.program_id(0) > 0)
    def _():
        for part in range(2):
            out[part] = base[part] - scale * acc[0, part]


def update(base, acc, weight, extra):
    chunks = weight.shape[0]
    tile = pl.BlockSpec((2, SIDE, SIDE), lambda i: (0, 0, i))
    return pl.pallas_call(
        update_kernel,
        grid=(chunks,),
        in_specs=[
            tile,
            pl.BlockSpec((1, 2, SIDE, SIDE), lambda i: (i, 0, 0, 0)),
            pl.BlockSpec((1, SIDE, SIDE), lambda i: (i, 0, 0)),
            pl.BlockSpec((2, SIDE, SIDE), lambda i: (0, 0, 0)),
        ],
        out_specs=tile,
        out_shape=jax.ShapeDtypeStruct(base.shape, f32),
        name="update",
    )(base, acc, weight, extra)


def shards(object_field, probe_modes, offsets, live_counts, patterns):
    tile_rows, tile_cols = object_field.shape[1:]
    chunks = tile_cols // SIDE
    batches, capacity = offsets.shape[:2]
    mats = jnp.asarray(matrices())
    anchor = jnp.stack([lax.axis_index("row") * tile_rows, lax.axis_index("col") * tile_cols])
    local = offsets - anchor[None, None, :]
    row_at, col_at = local[..., 0], local[..., 1]
    live = (jnp.arange(capacity)[None, :] < live_counts).astype(jnp.int32)
    own = jnp.stack([col_at // SIDE, row_at, col_at % SIDE, live], axis=-1)
    two = jnp.stack([own, shifted(own, "row", 1)], axis=1)
    infos = jnp.concatenate([two, shifted(two, "col", 1)], axis=1)
    ordered = [order_patterns(patterns[b]) for b in range(batches)]

    tile, probe = object_field, probe_modes
    rim = shifted(tile[:, :, :SIDE], "col", -1)
    for b in range(batches):
        info = infos[b]
        below = [shifted(pack(info[1, s], tile, rim), "row", -1) for s in range(capacity)]
        base, weight = prepare(info, tile, rim, probe)
        if b + 1 < batches:
            side = jnp.concatenate([base[:, :, :SIDE], weight[:1]], axis=0)
            side = shifted(side, "col", -1)
        pg, own_grads, arrived = None, [], []
        for s in range(capacity):
            grad, pg = run_slot(info[0, s], s, tile, rim, below[s], ordered[b], probe, mats, pg)
            own_grads.append(grad)
            arrived.append(shifted(grad, "row", 1))
        acc = gather(info, own_grads, arrived, chunks)
        from_left = shifted(acc[chunks], "col", 1)
        if b + 1 < batches:
            from_right = shifted(acc[0], "col", -1)
            rim = side[:2] - step_object * (acc[chunks] + from_right) / (side[2] + object_floor)
        tile = update(base, acc, weight, from_left)
        total = lax.psum(pg, ("row", "col"))
        step = step_probe * total[: 2 * MODES] / (total[2 * MODES] + probe_floor)
        probe = probe - step.reshape(probe.shape)
    return (tile, probe)


def solution(mesh):
    placed = (
        P(None, "row", "col"),
        P(),
        P(None, ("row", "col"), None),
        P(None, ("row", "col")),
        P(None, ("row", "col"), None, None),
    )
    return jax.shard_map(
        shards, mesh=mesh, in_specs=placed, out_specs=(P(None, "row", "col"), P()), check_vma=False
    )
```

time: 1090 us -> 500 us (0.46)
  waiting for transfers between devices: 553 us -> 284 us
  starting transfers between devices: 261 us -> 88 us
  matrix products: 89.7 us -> 0 us
  Pallas kernels: 0 us -> 70.5 us
  local copies, waits for them, and re-layouts: 89.3 us -> 22.1 us
  other arithmetic: 45.1 us -> 13.6 us
  loops' own time: 26.4 us -> 0 us
    ppermute x8 -> x25, starting transfers between devices: 238 us -> 87.9 us  [shifted(): lax.ppermute(value, axis, [(source, source + steps) for source in range(l...]
    ppermute x8 -> x25, waiting for transfers between devices: 208 us -> 65.4 us  [shifted(): lax.ppermute(value, axis, [(source, source + steps) for source in range(l...]
    psum x2, waiting for transfers between devices: 341 us -> 219 us  [shards(): total = lax.psum(pg, ('row', 'col'))]
    dot_general x32 -> x0, matrix products: 89.7 us -> none  [the longest x16 45.9 us: apply_columns(): return jnp.einsum('mjk,kl->mjl', values, matrix, precision=highest)]
    pallas_call x0 -> x20, Pallas kernels: none -> 70.5 us  [the longest x6 25 us: run_slot(): pl.pallas_call(lambda *refs: slot_kernel(last, first, *refs), grid_spec=p...]
    another operation x6 -> x0, loops' own time: 26.4 us -> none  [the longest x2 16.1 us: run_items(): return lax.fori_loop(first_item, last_item, visit_item, start_state)]
    gather x18 -> x0, local copies, waits for them, and re-layouts: 24.3 us -> none
    ppermute x8 -> x0, starting transfers between devices: 22.9 us -> none  [the longest x4 15.1 us: padded(): before = lax.ppermute(last, axis, up)]
  transfers between devices with their start and end apart: 18 -> 27, of which waited for: 12 -> 12; matrix products, arithmetic and copies ran while one was open for 2% -> 3% of each run, Pallas kernels for 0% -> 13%
where the time goes in v1:
time: 500 us; the launch traced here: 493 us
  waiting for transfers between devices  284 us (57%)
  starting transfers between devices  88 us (18%)
  Pallas kernels  70.5 us (14%)
  local copies, waits for them, and re-layouts  22.1 us (4%)
  between operations  14.8 us (3%)
  other arithmetic  13.6 us (3%)
    psum x2, waiting for transfers between devices, shards(): total = lax.psum(pg, ('row', 'col'))  219 us
    ppermute x25, starting transfers between devices, shifted(): lax.ppermute(value, axis, [(source, source + steps) for source in range(l...  87.9 us
    ppermute x25, waiting for transfers between devices, shifted(): lax.ppermute(value, axis, [(source, source + steps) for source in range(l...  65.4 us
    pallas_call x6, Pallas kernels, run_slot(): pl.pallas_call(lambda *refs: slot_kernel(last, first, *refs), grid_spec=p...  25 us
    pallas_call x6, Pallas kernels, pack(): pl.pallas_call(lambda *refs: pack_kernel(last, *refs), grid_spec=pltpu.Pr...  18 us
    unnamed x56, local copies, waits for them, and re-layouts  15.3 us
  transfers between devices with their start and end apart: 27, of which 12 were waited for; matrix products, arithmetic and copies ran while one was open for 3% of the time, Pallas kernels for 13%

profile of v1, /device:TPU:1, one launch (start us, length us, event | category | flops | bytes accessed | tf_op | source)
XLA Modules:
  0.0 492.9 jit_solution(13587482623776742601)
XLA Ops:
  8.8 3.9 collective-permute-start
  13.6 4.9 %collective-permute-start.1 = (s32[2,2,3,4]{3,0,2,1:T(2,128)S(1)}, s32[2,2,3,4]{3,0,2,1:T(2,128)S(1)}, u32[]{:S(2)}, u32[]{:S(2)}) collective-permute-start(s32[2,2,3,4]{3,0,2,1:T(2,128)S(1)} %pad_add_fusion.1), channel_id=1, source_target_pairs={{0,1},{1,2},{2,3},{3,4},{4,5},{5,6},{6,7},{8,9},{9,10},{10,11},{11... | collective-permute-start | bytes 584 | tf_op jit(solution)/shard_map/ppermute | solution.py:27
  22.2 7.9 %collective-permute-done.5.rim.refs_3_ = f32[2,256,256]{2,1,0:T(8,128)S(1)} collective-permute-done((f32[2,256,256]{2,1,0:T(8,128)S(1)}, f32[2,256,256]{2,1,0:T(8,128)S(1)}, u32[]{:S(2)}, u32[]{:S(2)}) %collective-permute-start.5) | collective-permute-done | bytes 524320 | tf_op jit(solution)/shard_map/ppermute | solution.py:27
  38.7 3.0 pack.7
  44.3 3.7 order_patterns.2.refs_5_
  48.0 3.2 pack.8
  55.4 8.3 %slot.6 = (f32[2,256,256]{2,1,0:T(8,128)}, f32[9,256,256]{2,1,0:T(8,128)S(1)}) custom-call(s32[4]{0:T(128)S(1)} %get-tuple-element.57.refs_0_, f32[2,256,1024]{2,1,0:T(8,128)S(1)} %copy-done.1, f32[2,256,1024]{2,1,0:T(8,128)S(1)} %copy-done.1, f32[2,256,256]{2,1,0:T(8,128)S(1)} %copy-done.12, f32[2,256,256]{2,1,0:T(8,128)} %collective-permute-done.6.refs_4_, ...), custom_call_target="tpu_custom_call" | custom-call | flops 3221225472 | bytes 8388608 | tf_op jit(solution)/shard_map/slot/pallas_call | solution.py:200
  70.8 14.8 %collective-permute-start.11 = (f32[2,256,256]{2,1,0:T(8,128)}, f32[2,256,256]{2,1,0:T(8,128)S(1)}, u32[]{:S(2)}, u32[]{:S(2)}) collective-permute-start(f32[2,256,256]{2,1,0:T(8,128)} %get-tuple-element.23.refs_2_), channel_id=1, source_target_pairs={{0,8},{8,16},{16,24},{24,32},{32,40},{40,48},{48,56},{56,64},{64,7... | collective-permute-start | bytes 1572872 | tf_op jit(solution)/shard_map/ppermute | solution.py:27
  85.6 4.3 collective-permute-start.10
  89.9 3.4 collective-permute-start.9
  94.6 3.7 collective-permute-done.3.below
  99.9 19.8 %collective-permute-done.2.above = f32[2,8,1024]{2,1,0:T(8,128)S(1)} collective-permute-done((f32[2,8,1024]{2,1,0:T(8,128)S(1)}, f32[2,8,1024]{2,1,0:T(8,128)S(1)}, u32[]{:S(2)}, u32[]{:S(2)}) %collective-permute-start.2) | collective-permute-done | bytes 65568 | tf_op jit(solution)/shard_map/ppermute | solution.py:27
  119.7 3.2 prepare.2
  125.2 4.4 collective-permute-start.16
  134.8 3.2 collective-permute-start.17
  138.0 3.8 order_patterns.3.refs_5_
  143.4 4.8 update.2.tile.refs_1_.refs_2_
  150.5 3.0 pack.11
  153.5 2.9 pack.10
  156.4 2.9 pack.9
  163.2 123.9 %all-reduce.3.cloned.1.call-done = f32[9,256,256]{2,1,0:T(8,128)} async-done(((f32[9,256,256]{2,1,0:T(8,128)}), f32[9,256,256]{2,1,0:T(8,128)}) %all-reduce.3.cloned.1.call-update) | async-done | bytes 2359312 | tf_op jit(solution)/shard_map/psum | solution.py:385
  294.6 6.8 %slot.9 = (f32[2,256,256]{2,1,0:T(8,128)S(1)}, f32[9,256,256]{2,1,0:T(8,128)S(1)}) custom-call(s32[4]{0:T(128)S(1)} %get-tuple-element.51.refs_0_, f32[2,256,1024]{2,1,0:T(8,128)S(1)} %copy-done, f32[2,256,1024]{2,1,0:T(8,128)S(1)} %copy-done, f32[2,256,256]{2,1,0:T(8,128)S(1)} %copy-done.6, f32[2,256,256]{2,1,0:T(8,128)S(1)} %copy-done.22, ...), custom_call_target="tpu_custom_call" | custom-call | flops 3221225472 | bytes 8388608 | tf_op jit(solution)/shard_map/slot/pallas_call | solution.py:200
  301.4 3.0 slot.10
  308.3 15.0 %collective-permute-start.23 = (f32[2,256,256]{2,1,0:T(8,128)}, f32[2,256,256]{2,1,0:T(8,128)}, u32[]{:S(2)}, u32[]{:S(2)}) collective-permute-start(f32[2,256,256]{2,1,0:T(8,128)} %get-tuple-element.31.refs_2_), channel_id=1, source_target_pairs={{0,8},{8,16},{16,24},{24,32},{32,40},{40,48},{48,56},{56,64},{64,7... | collective-permute-start | bytes 1572872 | tf_op jit(solution)/shard_map/ppermute | solution.py:27
  323.3 3.2 collective-permute-start.22
  328.6 3.8 collective-permute-done.23.refs_5_
  332.4 12.3 %collective-permute-done.22.refs_4_ = f32[2,256,256]{2,1,0:T(8,128)} collective-permute-done((f32[2,256,256]{2,1,0:T(8,128)}, f32[2,256,256]{2,1,0:T(8,128)}, u32[]{:S(2)}, u32[]{:S(2)}) %collective-permute-start.22) | collective-permute-done | bytes 524320 | tf_op jit(solution)/shard_map/ppermute | solution.py:27
  344.7 13.2 %collective-permute-done.21.refs_3_ = f32[2,256,256]{2,1,0:T(8,128)} collective-permute-done((f32[2,256,256]{2,1,0:T(8,128)S(1)}, f32[2,256,256]{2,1,0:T(8,128)}, u32[]{:S(2)}, u32[]{:S(2)}) %collective-permute-start.21) | collective-permute-done | bytes 524320 | tf_op jit(solution)/shard_map/ppermute | solution.py:27
  361.8 4.0 collective-permute-start.24
  369.1 5.2 %collective-permute-start.13 = (f32[2,8,1024]{2,1,0:T(8,128)S(1)}, f32[2,8,1024]{2,1,0:T(8,128)S(1)}, u32[]{:S(2)}, u32[]{:S(2)}) collective-permute-start(f32[2,8,1024]{2,1,0:T(8,128)S(1)} %get-tuple-element.39), channel_id=1, source_target_pairs={{0,8},{8,16},{16,24},{24,32},{32,40},{40,48},{48,56},{56,64},{64,7... | collective-permute-start | bytes 196616 | tf_op jit(solution)/shard_map/ppermute | solution.py:27
  381.6 4.8 update.3
  386.4 94.6 %all-reduce.5.cloned.1.call-done = f32[9,256,256]{2,1,0:T(8,128)} async-done(((f32[9,256,256]{2,1,0:T(8,128)}), f32[9,256,256]{2,1,0:T(8,128)}) %all-reduce.5.cloned.1.call-update) | async-done | bytes 2359312 | tf_op jit(solution)/shard_map/psum | solution.py:385
  (135 shorter events, 79.2 us)
Async XLA Ops:
  7.2 280.0 %all-reduce.3.cloned.1.call-start = ((), (), s32[]{:S(2)}) async-start(), calls=%async_computation | async-start | bytes 4718592 | tf_op jit(solution)/shard_map/psum | solution.py:385
  8.8 4.7 collective-permute-start
  13.6 8.0 %collective-permute-start.1 = (s32[2,2,3,4]{3,0,2,1:T(2,128)S(1)}, s32[2,2,3,4]{3,0,2,1:T(2,128)S(1)}, u32[]{:S(2)}, u32[]{:S(2)}) collective-permute-start(s32[2,2,3,4]{3,0,2,1:T(2,128)S(1)} %pad_add_fusion.1), channel_id=1, source_target_pairs={{0,1},{1,2},{2,3},{3,4},{4,5},{5,6},{6,7},{8,9},{9,10},{10,11},{11... | collective-permute-start | bytes 584 | tf_op jit(solution)/shard_map/ppermute | solution.py:27
  19.6 10.5 %collective-permute-start.5 = (f32[2,256,256]{2,1,0:T(8,128)S(1)}, f32[2,256,256]{2,1,0:T(8,128)S(1)}, u32[]{:S(2)}, u32[]{:S(2)}) collective-permute-start(f32[2,256,256]{2,1,0:T(8,128)S(1)} %slice.116), channel_id=1, source_target_pairs={{1,0},{2,1},{3,2},{4,3},{5,4},{6,5},{7,6},{9,8},{10,9},{11,10},{12... | collective-permute-start | bytes 1572872 | tf_op jit(solution)/shard_map/ppermute | solution.py:27
  33.8 18.7 %collective-permute-start.6 = (f32[2,256,256]{2,1,0:T(8,128)}, f32[2,256,256]{2,1,0:T(8,128)}, u32[]{:S(2)}, u32[]{:S(2)}) collective-permute-start(f32[2,256,256]{2,1,0:T(8,128)} %pack.6), channel_id=1, source_target_pairs={{8,0},{16,8},{24,16},{32,24},{40,32},{48,40},{56,48},{64,56},{72,6... | collective-permute-start | bytes 1572872 | tf_op jit(solution)/shard_map/ppermute | solution.py:27
  36.8 82.9 %collective-permute-start.4 = (f32[2,256,128]{2,1,0:T(8,128)}, f32[2,256,128]{2,1,0:T(8,128)}, u32[]{:S(2)}, u32[]{:S(2)}) collective-permute-start(f32[2,256,128]{2,1,0:T(8,128)} %slice.115), channel_id=1, source_target_pairs={{0,1},{1,2},{2,3},{3,4},{4,5},{5,6},{6,7},{8,9},{9,10},{10,11},{11... | collective-permute-start | bytes 786440 | tf_op jit(solution)/shard_map/ppermute | solution.py:27
  41.7 22.0 %collective-permute-start.7 = (f32[2,256,256]{2,1,0:T(8,128)}, f32[2,256,256]{2,1,0:T(8,128)}, u32[]{:S(2)}, u32[]{:S(2)}) collective-permute-start(f32[2,256,256]{2,1,0:T(8,128)} %pack.7), channel_id=1, source_target_pairs={{8,0},{16,8},{24,16},{32,24},{40,32},{48,40},{56,48},{64,56},{72,6... | collective-permute-start | bytes 1572872 | tf_op jit(solution)/shard_map/ppermute | solution.py:27
  51.3 17.9 %collective-permute-start.8 = (f32[2,256,256]{2,1,0:T(8,128)}, f32[2,256,256]{2,1,0:T(8,128)S(1)}, u32[]{:S(2)}, u32[]{:S(2)}) collective-permute-start(f32[2,256,256]{2,1,0:T(8,128)} %pack.8), channel_id=1, source_target_pairs={{8,0},{16,8},{24,16},{32,24},{40,32},{48,40},{56,48},{64,56},{72,6... | collective-permute-start | bytes 1572872 | tf_op jit(solution)/shard_map/ppermute | solution.py:27
  69.2 50.5 %copy-start.9 = (f32[4,2,256,256]{3,2,1,0:T(8,128)S(1)}, f32[4,2,256,256]{3,2,1,0:T(8,128)}, u32[]{:S(2)}) copy-start(f32[4,2,256,256]{3,2,1,0:T(8,128)} %refs_6_.5) | copy-start | bytes 6291460
  70.8 53.4 %copy-start.14 = (f32[9,256,256]{2,1,0:T(8,128)}, f32[9,256,256]{2,1,0:T(8,128)S(1)}, u32[]{:S(2)}) copy-start(f32[9,256,256]{2,1,0:T(8,128)S(1)} %get-tuple-element.25) | copy-start | bytes 7077892
  70.8 58.9 %collective-permute-start.11 = (f32[2,256,256]{2,1,0:T(8,128)}, f32[2,256,256]{2,1,0:T(8,128)S(1)}, u32[]{:S(2)}, u32[]{:S(2)}) collective-permute-start(f32[2,256,256]{2,1,0:T(8,128)} %get-tuple-element.23.refs_2_), channel_id=1, source_target_pairs={{0,8},{8,16},{16,24},{24,32},{32,40},{40,48},{48,56},{56,64},{64,7... | collective-permute-start | bytes 1572872 | tf_op jit(solution)/shard_map/ppermute | solution.py:27
  85.6 44.1 %collective-permute-start.10 = (f32[2,256,256]{2,1,0:T(8,128)}, f32[2,256,256]{2,1,0:T(8,128)}, u32[]{:S(2)}, u32[]{:S(2)}) collective-permute-start(f32[2,256,256]{2,1,0:T(8,128)} %get-tuple-element.21.refs_1_), channel_id=1, source_target_pairs={{0,8},{8,16},{16,24},{24,32},{32,40},{40,48},{48,56},{56,64},{64,7... | collective-permute-start | bytes 1572872 | tf_op jit(solution)/shard_map/ppermute | solution.py:27
  89.9 39.8 %collective-permute-start.9 = (f32[2,256,256]{2,1,0:T(8,128)}, f32[2,256,256]{2,1,0:T(8,128)}, u32[]{:S(2)}, u32[]{:S(2)}) collective-permute-start(f32[2,256,256]{2,1,0:T(8,128)} %get-tuple-element.19.refs_0_), channel_id=1, source_target_pairs={{0,8},{8,16},{16,24},{24,32},{32,40},{40,48},{48,56},{56,64},{64,7... | collective-permute-start | bytes 1572872 | tf_op jit(solution)/shard_map/ppermute | solution.py:27
  93.3 5.0 %collective-permute-start.3 = (f32[2,8,1024]{2,1,0:T(8,128)S(1)}, f32[2,8,1024]{2,1,0:T(8,128)S(1)}, u32[]{:S(2)}, u32[]{:S(2)}) collective-permute-start(f32[2,8,1024]{2,1,0:T(8,128)S(1)} %get-tuple-element.40), channel_id=1, source_target_pairs={{8,0},{16,8},{24,16},{32,24},{40,32},{48,40},{56,48},{64,56},{72,6... | collective-permute-start | bytes 196616 | tf_op jit(solution)/shard_map/ppermute | solution.py:27
  98.3 21.4 %collective-permute-start.2 = (f32[2,8,1024]{2,1,0:T(8,128)S(1)}, f32[2,8,1024]{2,1,0:T(8,128)S(1)}, u32[]{:S(2)}, u32[]{:S(2)}) collective-permute-start(f32[2,8,1024]{2,1,0:T(8,128)S(1)} %get-tuple-element.41), channel_id=1, source_target_pairs={{0,8},{8,16},{16,24},{24,32},{32,40},{40,48},{48,56},{56,64},{64,7... | collective-permute-start | bytes 196616 | tf_op jit(solution)/shard_map/ppermute | solution.py:27
  125.2 17.2 %collective-permute-start.16 = (f32[3,256,256]{2,1,0:T(8,128)}, f32[3,256,256]{2,1,0:T(8,128)}, u32[]{:S(2)}, u32[]{:S(2)}) collective-permute-start(f32[3,256,256]{2,1,0:T(8,128)} %pad_maximum_fusion), channel_id=1, source_target_pairs={{1,0},{2,1},{3,2},{4,3},{5,4},{6,5},{7,6},{9,8},{10,9},{11,10},{12... | collective-permute-start | bytes 2359304 | tf_op jit(solution)/shard_map/ppermute | solution.py:27
  129.6 351.4 %all-reduce.5.cloned.1.call-start = ((), (), s32[]{:S(2)}) async-start(), calls=%async_computation.1 | async-start | bytes 4718592 | tf_op jit(solution)/shard_map/psum | solution.py:385
  131.7 11.7 %copy-start.5 = (f32[5,2,256,256]{3,2,1,0:T(8,128)}, f32[5,2,256,256]{3,2,1,0:T(8,128)S(1)}, u32[]{:S(2)}) copy-start(f32[5,2,256,256]{3,2,1,0:T(8,128)S(1)} %gather.2.acc) | copy-start | bytes 7864324
  132.9 10.5 %collective-permute-start.12 = (f32[2,256,256]{2,1,0:T(8,128)}, f32[2,256,256]{2,1,0:T(8,128)}, u32[]{:S(2)}, u32[]{:S(2)}) collective-permute-start(f32[2,256,256]{2,1,0:T(8,128)} %get-tuple-element.37), channel_id=1, source_target_pairs={{0,1},{1,2},{2,3},{3,4},{4,5},{5,6},{6,7},{8,9},{9,10},{10,11},{11... | collective-permute-start | bytes 1572872 | tf_op jit(solution)/shard_map/ppermute | solution.py:27
  134.8 13.4 %collective-permute-start.17 = (f32[2,256,256]{2,1,0:T(8,128)}, f32[2,256,256]{2,1,0:T(8,128)}, u32[]{:S(2)}, u32[]{:S(2)}) collective-permute-start(f32[2,256,256]{2,1,0:T(8,128)} %get-tuple-element.36), channel_id=1, source_target_pairs={{1,0},{2,1},{3,2},{4,3},{5,4},{6,5},{7,6},{9,8},{10,9},{11,10},{12... | collective-permute-start | bytes 1572872 | tf_op jit(solution)/shard_map/ppermute | solution.py:27
  159.4 131.3 %collective-permute-start.18 = (f32[2,256,256]{2,1,0:T(8,128)}, f32[2,256,256]{2,1,0:T(8,128)S(1)}, u32[]{:S(2)}, u32[]{:S(2)}) collective-permute-start(f32[2,256,256]{2,1,0:T(8,128)} %pack.9), channel_id=1, source_target_pairs={{8,0},{16,8},{24,16},{32,24},{40,32},{48,40},{56,48},{64,56},{72,6... | collective-permute-start | bytes 1572872 | tf_op jit(solution)/shard_map/ppermute | solution.py:27
  160.6 140.7 %collective-permute-start.19 = (f32[2,256,256]{2,1,0:T(8,128)}, f32[2,256,256]{2,1,0:T(8,128)}, u32[]{:S(2)}, u32[]{:S(2)}) collective-permute-start(f32[2,256,256]{2,1,0:T(8,128)} %pack.10), channel_id=1, source_target_pairs={{8,0},{16,8},{24,16},{32,24},{40,32},{48,40},{56,48},{64,56},{72,6... | collective-permute-start | bytes 1572872 | tf_op jit(solution)/shard_map/ppermute | solution.py:27
  161.9 142.4 %collective-permute-start.20 = (f32[2,256,256]{2,1,0:T(8,128)}, f32[2,256,256]{2,1,0:T(8,128)}, u32[]{:S(2)}, u32[]{:S(2)}) collective-permute-start(f32[2,256,256]{2,1,0:T(8,128)} %pack.11), channel_id=1, source_target_pairs={{8,0},{16,8},{24,16},{32,24},{40,32},{48,40},{56,48},{64,56},{72,6... | collective-permute-start | bytes 1572872 | tf_op jit(solution)/shard_map/ppermute | solution.py:27
  290.6 13.7 %copy-start.2 = (f32[4,2,256,256]{3,2,1,0:T(8,128)}, f32[4,2,256,256]{3,2,1,0:T(8,128)S(1)}, u32[]{:S(2)}) copy-start(f32[4,2,256,256]{3,2,1,0:T(8,128)S(1)} %sub.25.probe_ref.refs_6_) | copy-start | bytes 6291460
  308.3 24.1 %collective-permute-start.23 = (f32[2,256,256]{2,1,0:T(8,128)}, f32[2,256,256]{2,1,0:T(8,128)}, u32[]{:S(2)}, u32[]{:S(2)}) collective-permute-start(f32[2,256,256]{2,1,0:T(8,128)} %get-tuple-element.31.refs_2_), channel_id=1, source_target_pairs={{0,8},{8,16},{16,24},{24,32},{32,40},{40,48},{48,56},{56,64},{64,7... | collective-permute-start | bytes 1572872 | tf_op jit(solution)/shard_map/ppermute | solution.py:27
  323.3 21.4 %collective-permute-start.22 = (f32[2,256,256]{2,1,0:T(8,128)}, f32[2,256,256]{2,1,0:T(8,128)}, u32[]{:S(2)}, u32[]{:S(2)}) collective-permute-start(f32[2,256,256]{2,1,0:T(8,128)} %get-tuple-element.29.refs_1_), channel_id=1, source_target_pairs={{0,8},{8,16},{16,24},{24,32},{32,40},{40,48},{48,56},{56,64},{64,7... | collective-permute-start | bytes 1572872 | tf_op jit(solution)/shard_map/ppermute | solution.py:27
  326.5 31.4 %collective-permute-start.21 = (f32[2,256,256]{2,1,0:T(8,128)S(1)}, f32[2,256,256]{2,1,0:T(8,128)}, u32[]{:S(2)}, u32[]{:S(2)}) collective-permute-start(f32[2,256,256]{2,1,0:T(8,128)S(1)} %get-tuple-element.27.refs_0_), channel_id=1, source_target_pairs={{0,8},{8,16},{16,24},{24,32},{32,40},{40,48},{48,56},{56,64},{64,7... | collective-permute-start | bytes 1572872 | tf_op jit(solution)/shard_map/ppermute | solution.py:27
  358.0 17.7 %copy-start.3 = (f32[4,2,256,256]{3,2,1,0:T(8,128)S(1)}, f32[4,2,256,256]{3,2,1,0:T(8,128)}, u32[]{:S(2)}) copy-start(f32[4,2,256,256]{3,2,1,0:T(8,128)} %copy-done.2) | copy-start | bytes 6291460
  361.8 19.0 %collective-permute-start.24 = (f32[2,256,256]{2,1,0:T(8,128)S(1)}, f32[2,256,256]{2,1,0:T(8,128)S(1)}, u32[]{:S(2)}, u32[]{:S(2)}) collective-permute-start(f32[2,256,256]{2,1,0:T(8,128)S(1)} %slice_bitcast_fusion.2), channel_id=1, source_target_pairs={{0,1},{1,2},{2,3},{3,4},{4,5},{5,6},{6,7},{8,9},{9,10},{10,11},{11... | collective-permute-start | bytes 1572872 | tf_op jit(solution)/shard_map/ppermute | solution.py:27
  365.9 9.7 %collective-permute-start.15 = (f32[2,256,128]{2,1,0:T(8,128)S(1)}, f32[2,256,128]{2,1,0:T(8,128)S(1)}, u32[]{:S(2)}, u32[]{:S(2)}) collective-permute-start(f32[2,256,128]{2,1,0:T(8,128)S(1)} %slice.158), channel_id=1, source_target_pairs={{0,1},{1,2},{2,3},{3,4},{4,5},{5,6},{6,7},{8,9},{9,10},{10,11},{11... | collective-permute-start | bytes 786440 | tf_op jit(solution)/shard_map/ppermute | solution.py:27
  367.8 6.5 %collective-permute-start.14 = (f32[2,8,1024]{2,1,0:T(8,128)S(1)}, f32[2,8,1024]{2,1,0:T(8,128)S(1)}, u32[]{:S(2)}, u32[]{:S(2)}) collective-permute-start(f32[2,8,1024]{2,1,0:T(8,128)S(1)} %get-tuple-element.38), channel_id=1, source_target_pairs={{8,0},{16,8},{24,16},{32,24},{40,32},{48,40},{56,48},{64,56},{72,6... | collective-permute-start | bytes 196616 | tf_op jit(solution)/shard_map/ppermute | solution.py:27
  369.1 6.5 %collective-permute-start.13 = (f32[2,8,1024]{2,1,0:T(8,128)S(1)}, f32[2,8,1024]{2,1,0:T(8,128)S(1)}, u32[]{:S(2)}, u32[]{:S(2)}) collective-permute-start(f32[2,8,1024]{2,1,0:T(8,128)S(1)} %get-tuple-element.39), channel_id=1, source_target_pairs={{0,8},{8,16},{16,24},{24,32},{32,40},{40,48},{48,56},{56,64},{64,7... | collective-permute-start | bytes 196616 | tf_op jit(solution)/shard_map/ppermute | solution.py:27
  (23 other events, 54.0 us)
Sparse Core Ops, SparseCore 0:
  129.7 157.3 all-reduce.2
  328.7 152.2 all-reduce.4

commit v2 on v1

--- a/solution.py
+++ b/solution.py
@@ -348,6 +348,177 @@
     )(base, acc, weight, extra)
 
 
+MESH = pl.DeviceIdType.MESH
+PLANES = 2 * MODES + 1
+
+
+def place():
+    row, col = lax.axis_index("row"), lax.axis_index("col")
+    return lax.div(row, 4), lax.rem(row, 4), lax.div(col, 2), lax.rem(col, 2)
+
+
+def device(y, x, z, core):
+    return (y * 4 + x, z * 2 + core)
+
+
+def peers(y, x, z, core, axis, step):
+    if axis == "core":
+        return device(y, x, z, 1 - core)
+    if axis == "x":
+        return device(y, lax.rem(x + step, 4), z, core)
+    along_y = (1 - core) if axis == "first" else core
+    return device(lax.rem(y + step * along_y, 4), x, lax.rem(z + step * (1 - along_y), 4), core)
+
+
+def meet(here, axes):
+    barrier = pltpu.get_barrier_semaphore()
+    who = [peers(*here, axis, step) for axis in axes for step in ((1,) if axis == "core" else (1, 2, 3))]
+    for device_id in who:
+        pl.semaphore_signal(barrier, inc=1, device_id=device_id, device_id_type=MESH)
+    pl.semaphore_wait(barrier, len(who))
+
+
+def remote(src, dst, send, recv, device_id):
+    return pltpu.make_async_remote_copy(
+        src_ref=src, dst_ref=dst, send_sem=send, recv_sem=recv, device_id=device_id, device_id_type=MESH
+    )
+
+
+def reduce_kernel(pg, probe, out, half, got1, got2, got3, got4, send, recv):
+    here = y, x, z, core = place()
+    first, second = y + core * (z - y), z + core * (y - z)
+    meet(here, ("core", "first", "second", "x"))
+    sibling = peers(*here, "core", 1)
+    order = [lax.rem(first + step, 4) for step in (2, 1, 3, 0)]
+    at = lambda base, index, size: pl.ds(pl.multiple_of(base + index * size, 8), size)
+    ones = []
+    for i, piece in enumerate(order):
+        theirs = at((1 - core) * HALF, lax.rem(second + (2, 1, 3, 0)[i], 4), 32)
+        there = at(0, lax.rem(second + (2, 1, 3, 0)[i], 4), 32)
+        copy = remote(pg.at[:, theirs, :], got1.at[:, there, :], send.at[i], recv.at[i], sibling)
+        copy.start()
+        ones.append(copy)
+    twos = []
+    for i, piece in enumerate(order):
+        ones[i].wait_recv()
+        mine, there = at(core * HALF, piece, 32), at(0, piece, 32)
+        half[:, there, :] = pg[:, mine, :] + got1[:, there, :]
+        if i < 3:
+            step = (2, 1, 3)[i]
+            copy = remote(
+                half.at[:, there, :], got2.at[step - 1], send.at[4 + i], recv.at[4 + i], peers(*here, "first", step)
+            )
+            copy.start()
+            twos.append(copy)
+    for copy in twos:
+        copy.wait_recv()
+    start = first * 32
+    threes = []
+    for i, step in enumerate((2, 1, 3, 0)):
+        piece = lax.rem(second + step, 4)
+        rows, within = at(start, piece, 8), at(0, piece, 8)
+        half[:, rows, :] = half[:, rows, :] + got2[0, :, within, :] + got2[1, :, within, :] + got2[2, :, within, :]
+        if step:
+            copy = remote(
+                half.at[:, rows, :], got3.at[step - 1], send.at[7 + i], recv.at[7 + i], peers(*here, "second", step)
+            )
+            copy.start()
+            threes.append(copy)
+    for copy in threes:
+        copy.wait_recv()
+    rows = at(start, second, 8)
+    got4[x] = half[:, rows, :] + got3[0] + got3[1] + got3[2]
+    fours = []
+    for i, step in enumerate((2, 1, 3)):
+        copy = remote(got4.at[x], got4.at[x], send.at[10 + i], recv.at[10 + i], peers(*here, "x", step))
+        copy.start()
+        fours.append(copy)
+    for copy in fours:
+        copy.wait_recv()
+    total = got4[0] + got4[1] + got4[2] + got4[3]
+    scale = step_probe / (total[2 * MODES] + probe_floor)
+    mine = at(core * HALF + start, second, 8)
+    for plane in range(2 * MODES):
+        out[plane] = probe[plane, mine, :] - scale * total[plane]
+    for copy in ones + twos + threes + fours:
+        copy.wait_send()
+
+
+def spread_kernel(shard, out, send, recv):
+    here = y, x, z, core = place()
+    first, second = y + core * (z - y), z + core * (y - z)
+    meet(here, ("core", "first", "second"))
+    at = lambda base, index, size: out.at[:, pl.ds(pl.multiple_of(base + index * size, 8), size), :]
+    base = core * HALF
+    mine = base + first * 32 + second * 8
+    out[:, pl.ds(pl.multiple_of(mine, 8), 8), :] = shard[...]
+    copies = []
+    for i, step in enumerate((2, 1, 3)):
+        block = at(mine, 0, 8)
+        copy = remote(block, block, send.at[i], recv.at[i], peers(*here, "second", step))
+        copy.start()
+        copies.append(copy)
+    for copy in copies:
+        copy.wait_recv()
+    whole = at(base, first, 32)
+    twos = []
+    for i, step in enumerate((2, 1, 3)):
+        copy = remote(whole, whole, send.at[3 + i], recv.at[3 + i], peers(*here, "first", step))
+        copy.start()
+        twos.append(copy)
+    sibling = peers(*here, "core", 1)
+    threes = [remote(whole, whole, send.at[6], recv.at[6], sibling)]
+    threes[0].start()
+    for i, step in ((1, 1), (2, 3), (0, 2)):
+        twos[i].wait_recv()
+        block = at(base, lax.rem(first + 4 - step, 4), 32)
+        copy = remote(block, block, send.at[7 + i], recv.at[7 + i], sibling)
+        copy.start()
+        threes.append(copy)
+    for copy in threes:
+        copy.wait_recv()
+    for copy in copies + twos + threes:
+        copy.wait_send()
+
+
+def reduce_probe(pg, probe):
+    vmem = pl.BlockSpec(memory_space=VMEM)
+    return pl.pallas_call(
+        reduce_kernel,
+        in_specs=[vmem, vmem],
+        out_specs=vmem,
+        out_shape=jax.ShapeDtypeStruct((2 * MODES, 8, SIDE), f32),
+        scratch_shapes=[
+            pltpu.VMEM((PLANES, HALF, SIDE), f32),
+            pltpu.VMEM((PLANES, HALF, SIDE), f32),
+            pltpu.VMEM((3, PLANES, 32, SIDE), f32),
+            pltpu.VMEM((3, PLANES, 8, SIDE), f32),
+            pltpu.VMEM((4, PLANES, 8, SIDE), f32),
+            pltpu.SemaphoreType.DMA((13,)),
+            pltpu.SemaphoreType.DMA((13,)),
+        ],
+        compiler_params=pltpu.CompilerParams(
+            collective_id=0, has_side_effects=True, vmem_limit_bytes=24 * 2**20
+        ),
+        name="reduce_probe",
+    )(pg, probe)
+
+
+def spread_probe(shard):
+    vmem = pl.BlockSpec(memory_space=VMEM)
+    return pl.pallas_call(
+        spread_kernel,
+        in_specs=[vmem],
+        out_specs=vmem,
+        out_shape=jax.ShapeDtypeStruct((2 * MODES, SIDE, SIDE), f32),
+        scratch_shapes=[pltpu.SemaphoreType.DMA((10,)), pltpu.SemaphoreType.DMA((10,))],
+        compiler_params=pltpu.CompilerParams(
+            collective_id=1, has_side_effects=True, vmem_limit_bytes=24 * 2**20
+        ),
+        name="spread_probe",
+    )(shard)
+
+
 def shards(object_field, probe_modes, offsets, live_counts, patterns):
     tile_rows, tile_cols = object_field.shape[1:]
     chunks = tile_cols // SIDE
@@ -382,9 +553,8 @@
             from_right = shifted(acc[0], "col", -1)
             rim = side[:2] - step_object * (acc[chunks] + from_right) / (side[2] + object_floor)
         tile = update(base, acc, weight, from_left)
-        total = lax.psum(pg, ("row", "col"))
-        step = step_probe * total[: 2 * MODES] / (total[2 * MODES] + probe_floor)
-        probe = probe - step.reshape(probe.shape)
+        shard = reduce_probe(pg, probe.reshape(2 * MODES, SIDE, SIDE))
+        probe = spread_probe(shard).reshape(probe.shape)
     return (tile, probe)
 
 

time: 500 us -> 364 us (0.73)
  waiting for transfers between devices: 284 us -> 50.7 us
  Pallas kernels: 70.5 us -> 194 us
  between operations: 14.8 us -> 1.63 us
  other arithmetic: 13.6 us -> 4.01 us
    psum x2 -> x0, waiting for transfers between devices: 219 us -> none  [shards(): total = lax.psum(pg, ('row', 'col'))]
    pallas_call x0 -> x4, Pallas kernels: none -> 129 us  [the longest x2 83.3 us: reduce_probe(): pl.pallas_call(reduce_kernel, in_specs=[vmem, vmem], out_specs=vmem, out_...]
    ppermute x25, waiting for transfers between devices: 65.4 us -> 50.7 us  [shifted(): lax.ppermute(value, axis, [(source, source + steps) for source in range(l...]
    div x4 -> x0, other arithmetic: 5.87 us -> none  [shards(): step = step_probe * total[:2 * MODES] / (total[2 * MODES] + probe_floor)]
    unnamed x56 -> x59, local copies, waits for them, and re-layouts: 15.3 us -> 16.2 us
  transfers between devices with their start and end apart: 27 -> 25, of which waited for: 12 -> 11; matrix products, arithmetic and copies ran while one was open for 3% -> 2% of each run, Pallas kernels for 13% -> 51%
where the time goes in v2:
time: 364 us; the launch traced here: 357 us
  Pallas kernels  194 us (53%)
  starting transfers between devices  83.5 us (23%)
  waiting for transfers between devices  50.7 us (14%)
  local copies, waits for them, and re-layouts  22.7 us (6%)
  other arithmetic  4.01 us (1%)
    ppermute x25, starting transfers between devices, shifted(): lax.ppermute(value, axis, [(source, source + steps) for source in range(l...  83.5 us
    pallas_call x2, Pallas kernels, reduce_probe(): pl.pallas_call(reduce_kernel, in_specs=[vmem, vmem], out_specs=vmem, out_...  83.3 us
    ppermute x25, waiting for transfers between devices, shifted(): lax.ppermute(value, axis, [(source, source + steps) for source in range(l...  50.7 us
    pallas_call x2, Pallas kernels, spread_probe(): pl.pallas_call(spread_kernel, in_specs=[vmem], out_specs=vmem, out_shape=...  45.4 us
    pallas_call x6, Pallas kernels, run_slot(): pl.pallas_call(lambda *refs: slot_kernel(last, first, *refs), grid_spec=p...  21.8 us
    pallas_call x6, Pallas kernels, pack(): pl.pallas_call(lambda *refs: pack_kernel(last, *refs), grid_spec=pltpu.Pr...  18.4 us
    unnamed x59, local copies, waits for them, and re-layouts  16.2 us
    pallas_call x2, Pallas kernels, update(): pl.pallas_call(update_kernel, grid=(chunks,), in_specs=[tile, pl.BlockSpe...  9.54 us
  transfers between devices with their start and end apart: 25, of which 11 were waited for; matrix products, arithmetic and copies ran while one was open for 2% of the time, Pallas kernels for 51%

profile of v2, /device:TPU:1, one launch (start us, length us, event | category | flops | bytes accessed | tf_op | source)
XLA Modules:
  0.0 356.5 jit_solution(6922253219586361973)
XLA Ops:
  2.2 3.9 %collective-permute-start = (s32[2,3,4]{1,2,0:T(4,128)S(1)}, s32[2,3,4]{1,2,0:T(4,128)S(1)}, u32[]{:S(2)}, u32[]{:S(2)}) collective-permute-start(s32[2,3,4]{1,2,0:T(4,128)S(1)} %pad_add_fusion.2), channel_id=1, source_target_pairs={{0,8},{8,16},{16,24},{24,32},{32,40},{40,48},{48,56},{56,64},{64,7... | collective-permute-start | bytes 296 | tf_op jit(solution)/shard_map/ppermute | solution.py:27
  7.0 4.9 %collective-permute-start.1 = (s32[2,2,3,4]{3,0,2,1:T(2,128)S(1)}, s32[2,2,3,4]{3,0,2,1:T(2,128)S(1)}, u32[]{:S(2)}, u32[]{:S(2)}) collective-permute-start(s32[2,2,3,4]{3,0,2,1:T(2,128)S(1)} %pad_add_fusion.1), channel_id=1, source_target_pairs={{0,1},{1,2},{2,3},{3,4},{4,5},{5,6},{6,7},{8,9},{9,10},{10,11},{11... | collective-permute-start | bytes 584 | tf_op jit(solution)/shard_map/ppermute | solution.py:27
  15.6 7.9 %collective-permute-done.5.rim.refs_3_ = f32[2,256,256]{2,1,0:T(8,128)S(1)} collective-permute-done((f32[2,256,256]{2,1,0:T(8,128)S(1)}, f32[2,256,256]{2,1,0:T(8,128)S(1)}, u32[]{:S(2)}, u32[]{:S(2)}) %collective-permute-start.5) | collective-permute-done | bytes 524320 | tf_op jit(solution)/shard_map/ppermute | solution.py:27
  32.2 3.0 pack.7
  37.7 3.7 %order_patterns.2.refs_5_ = f32[3,256,256]{2,1,0:T(8,128)} custom-call(f32[3,256,256]{2,1,0:T(8,128)} %get-tuple-element.43.pat_ref, bf16[2,256,256]{2,1,0:T(8,128)(2,1)} %constant.46.clone.perm_ref), custom_call_target="tpu_custom_call" | custom-call | tf_op jit(solution)/shard_map/order_patterns/pallas_call | solution.py:91
  41.5 3.2 pack.8
  48.9 7.8 %slot.6 = (f32[2,256,256]{2,1,0:T(8,128)S(1)}, f32[9,256,256]{2,1,0:T(8,128)S(1)}) custom-call(s32[4]{0:T(128)S(1)} %get-tuple-element.57.refs_0_, f32[2,256,1024]{2,1,0:T(8,128)S(1)} %copy-done.1, f32[2,256,1024]{2,1,0:T(8,128)S(1)} %copy-done.1, f32[2,256,256]{2,1,0:T(8,128)S(1)} %copy-done.12, f32[2,256,256]{2,1,0:T(8,128)} %collective-permute-done.6.refs_4_, ...), custom_call_target="tpu_custom_call" | custom-call | flops 3221225472 | bytes 8388608 | tf_op jit(solution)/shard_map/slot/pallas_call | solution.py:200
  58.7 4.0 %collective-permute-done.8.refs_4_ = f32[2,256,256]{2,1,0:T(8,128)S(1)} collective-permute-done((f32[2,256,256]{2,1,0:T(8,128)}, f32[2,256,256]{2,1,0:T(8,128)S(1)}, u32[]{:S(2)}, u32[]{:S(2)}) %collective-permute-start.8) | collective-permute-done | bytes 524320 | tf_op jit(solution)/shard_map/ppermute | solution.py:27
  64.9 3.5 collective-permute-start.11
  68.4 13.6 %collective-permute-start.10 = (f32[2,256,256]{2,1,0:T(8,128)S(1)}, f32[2,256,256]{2,1,0:T(8,128)S(1)}, u32[]{:S(2)}, u32[]{:S(2)}) collective-permute-start(f32[2,256,256]{2,1,0:T(8,128)S(1)} %get-tuple-element.21.refs_1_), channel_id=1, source_target_pairs={{0,8},{8,16},{16,24},{24,32},{32,40},{40,48},{48,56},{56,64},{64,7... | collective-permute-start | bytes 1572872 | tf_op jit(solution)/shard_map/ppermute | solution.py:27
  85.2 3.7 %collective-permute-done.3.below = f32[2,8,1024]{2,1,0:T(8,128)S(1)} collective-permute-done((f32[2,8,1024]{2,1,0:T(8,128)S(1)}, f32[2,8,1024]{2,1,0:T(8,128)S(1)}, u32[]{:S(2)}, u32[]{:S(2)}) %collective-permute-start.3) | collective-permute-done | bytes 65568 | tf_op jit(solution)/shard_map/ppermute | solution.py:27
  91.1 13.0 %collective-permute-done.2.above = f32[2,8,1024]{2,1,0:T(8,128)S(1)} collective-permute-done((f32[2,8,1024]{2,1,0:T(8,128)S(1)}, f32[2,8,1024]{2,1,0:T(8,128)S(1)}, u32[]{:S(2)}, u32[]{:S(2)}) %collective-permute-start.2) | collective-permute-done | bytes 65568 | tf_op jit(solution)/shard_map/ppermute | solution.py:27
  104.2 3.2 prepare.2
  107.5 4.4 %collective-permute-start.16 = (f32[3,256,256]{2,1,0:T(8,128)S(1)}, f32[3,256,256]{2,1,0:T(8,128)S(1)}, u32[]{:S(2)}, u32[]{:S(2)}) collective-permute-start(f32[3,256,256]{2,1,0:T(8,128)S(1)} %pad_maximum_fusion), channel_id=1, source_target_pairs={{1,0},{2,1},{3,2},{4,3},{5,4},{6,5},{7,6},{9,8},{10,9},{11,10},{12... | collective-permute-start | bytes 2359304 | tf_op jit(solution)/shard_map/ppermute | solution.py:27
  114.0 3.2 collective-permute-start.12
  119.7 3.2 collective-permute-done.16
  124.7 4.8 %update.2.tile.refs_1_.refs_2_ = f32[2,256,1024]{2,1,0:T(8,128)} custom-call(f32[2,256,1024]{2,1,0:T(8,128)} %copy-done.13, f32[5,2,256,256]{3,2,1,0:T(8,128)} %copy-done.5, f32[4,256,256]{2,1,0:T(8,128)} %copy-done.17, f32[2,256,256]{2,1,0:T(8,128)} %copy-done.28), custom_call_target="tpu_custom_call" | custom-call | tf_op jit(solution)/shard_map/update/pallas_call | solution.py:336
  136.0 3.0 pack.10
  140.3 3.8 %order_patterns.3.refs_5_ = f32[3,256,256]{2,1,0:T(8,128)} custom-call(f32[3,256,256]{2,1,0:T(8,128)} %get-tuple-element.42.pat_ref, bf16[2,256,256]{2,1,0:T(8,128)(2,1)} %constant.46.clone.perm_ref), custom_call_target="tpu_custom_call" | custom-call | tf_op jit(solution)/shard_map/order_patterns/pallas_call | solution.py:91
  145.7 42.7 %reduce_probe.2.shard = f32[8,8,256]{2,1,0:T(8,128)S(1)} custom-call(f32[9,256,256]{2,1,0:T(8,128)S(1)} %copy-done.15, f32[8,256,256]{2,1,0:T(8,128)S(1)} %bitcast.60), custom_call_target="tpu_custom_call" | custom-call | tf_op jit(solution)/shard_map/reduce_probe/pallas_call | solution.py:486
  188.5 28.2 %spread_probe.2.probe = f32[8,256,256]{2,1,0:T(8,128)S(1)} custom-call(f32[8,8,256]{2,1,0:T(8,128)S(1)} %reduce_probe.2.shard), custom_call_target="tpu_custom_call" | custom-call | tf_op jit(solution)/shard_map/spread_probe/pallas_call | solution.py:509
  218.0 3.3 pack.11
  225.4 8.4 %slot.9 = (f32[2,256,256]{2,1,0:T(8,128)S(1)}, f32[9,256,256]{2,1,0:T(8,128)S(1)}) custom-call(s32[4]{0:T(128)S(1)} %get-tuple-element.51.refs_0_, f32[2,256,1024]{2,1,0:T(8,128)S(1)} %copy-done, f32[2,256,1024]{2,1,0:T(8,128)S(1)} %copy-done, f32[2,256,256]{2,1,0:T(8,128)S(1)} %copy-done.6, f32[2,256,256]{2,1,0:T(8,128)} %collective-permute-done.18.refs_4_, ...), custom_call_target="tpu_custom_call" | custom-call | flops 3221225472 | bytes 8388608 | tf_op jit(solution)/shard_map/slot/pallas_call | solution.py:200
  237.7 3.0 collective-permute-start.23
  240.7 15.3 %collective-permute-start.22 = (f32[2,256,256]{2,1,0:T(8,128)S(1)}, f32[2,256,256]{2,1,0:T(8,128)S(1)}, u32[]{:S(2)}, u32[]{:S(2)}) collective-permute-start(f32[2,256,256]{2,1,0:T(8,128)S(1)} %get-tuple-element.29.refs_1_), channel_id=1, source_target_pairs={{0,8},{8,16},{16,24},{24,32},{32,40},{40,48},{48,56},{56,64},{64,7... | collective-permute-start | bytes 1572872 | tf_op jit(solution)/shard_map/ppermute | solution.py:27
  256.0 3.0 collective-permute-start.21
  259.0 8.7 %collective-permute-done.22.refs_4_ = f32[2,256,256]{2,1,0:T(8,128)S(1)} collective-permute-done((f32[2,256,256]{2,1,0:T(8,128)S(1)}, f32[2,256,256]{2,1,0:T(8,128)S(1)}, u32[]{:S(2)}, u32[]{:S(2)}) %collective-permute-start.22) | collective-permute-done | bytes 524320 | tf_op jit(solution)/shard_map/ppermute | solution.py:27
  267.8 7.1 %collective-permute-done.21.refs_3_ = f32[2,256,256]{2,1,0:T(8,128)S(1)} collective-permute-done((f32[2,256,256]{2,1,0:T(8,128)S(1)}, f32[2,256,256]{2,1,0:T(8,128)S(1)}, u32[]{:S(2)}, u32[]{:S(2)}) %collective-permute-start.21) | collective-permute-done | bytes 524320 | tf_op jit(solution)/shard_map/ppermute | solution.py:27
  282.6 4.7 %collective-permute-start.13 = (f32[2,8,1024]{2,1,0:T(8,128)S(1)}, f32[2,8,1024]{2,1,0:T(8,128)S(1)}, u32[]{:S(2)}, u32[]{:S(2)}) collective-permute-start(f32[2,8,1024]{2,1,0:T(8,128)S(1)} %get-tuple-element.39), channel_id=1, source_target_pairs={{0,8},{8,16},{16,24},{24,32},{32,40},{40,48},{48,56},{56,64},{64,7... | collective-permute-start | bytes 196616 | tf_op jit(solution)/shard_map/ppermute | solution.py:27
  291.5 40.6 %reduce_probe.3.shard = f32[8,8,256]{2,1,0:T(8,128)S(1)} custom-call(f32[9,256,256]{2,1,0:T(8,128)S(1)} %get-tuple-element.33.pg, f32[8,256,256]{2,1,0:T(8,128)S(1)} %copy-done.4), custom_call_target="tpu_custom_call" | custom-call | tf_op jit(solution)/shard_map/reduce_probe/pallas_call | solution.py:486
  332.1 17.3 %spread_probe.3 = f32[8,256,256]{2,1,0:T(8,128)S(1)} custom-call(f32[8,8,256]{2,1,0:T(8,128)S(1)} %reduce_probe.3.shard), custom_call_target="tpu_custom_call" | custom-call | tf_op jit(solution)/shard_map/spread_probe/pallas_call | solution.py:509
  350.2 4.8 %update.3 = f32[2,256,1024]{2,1,0:T(8,128)} custom-call(f32[2,256,1024]{2,1,0:T(8,128)} %copy-done.16, f32[5,2,256,256]{3,2,1,0:T(8,128)} %copy-done.7, f32[4,256,256]{2,1,0:T(8,128)} %copy-done.18, f32[2,256,256]{2,1,0:T(8,128)} %copy-done.27), custom_call_target="tpu_custom_call" | custom-call | tf_op jit(solution)/shard_map/update/pallas_call | solution.py:336
  (130 shorter events, 70.0 us)
Async XLA Ops:
  2.2 4.7 %collective-permute-start = (s32[2,3,4]{1,2,0:T(4,128)S(1)}, s32[2,3,4]{1,2,0:T(4,128)S(1)}, u32[]{:S(2)}, u32[]{:S(2)}) collective-permute-start(s32[2,3,4]{1,2,0:T(4,128)S(1)} %pad_add_fusion.2), channel_id=1, source_target_pairs={{0,8},{8,16},{16,24},{24,32},{32,40},{40,48},{48,56},{56,64},{64,7... | collective-permute-start | bytes 296 | tf_op jit(solution)/shard_map/ppermute | solution.py:27
  7.0 8.0 %collective-permute-start.1 = (s32[2,2,3,4]{3,0,2,1:T(2,128)S(1)}, s32[2,2,3,4]{3,0,2,1:T(2,128)S(1)}, u32[]{:S(2)}, u32[]{:S(2)}) collective-permute-start(s32[2,2,3,4]{3,0,2,1:T(2,128)S(1)} %pad_add_fusion.1), channel_id=1, source_target_pairs={{0,1},{1,2},{2,3},{3,4},{4,5},{5,6},{6,7},{8,9},{9,10},{10,11},{11... | collective-permute-start | bytes 584 | tf_op jit(solution)/shard_map/ppermute | solution.py:27
  13.1 10.5 %collective-permute-start.5 = (f32[2,256,256]{2,1,0:T(8,128)S(1)}, f32[2,256,256]{2,1,0:T(8,128)S(1)}, u32[]{:S(2)}, u32[]{:S(2)}) collective-permute-start(f32[2,256,256]{2,1,0:T(8,128)S(1)} %slice.104), channel_id=1, source_target_pairs={{1,0},{2,1},{3,2},{4,3},{5,4},{6,5},{7,6},{9,8},{10,9},{11,10},{12... | collective-permute-start | bytes 1572872 | tf_op jit(solution)/shard_map/ppermute | solution.py:27
  27.3 18.8 %collective-permute-start.6 = (f32[2,256,256]{2,1,0:T(8,128)}, f32[2,256,256]{2,1,0:T(8,128)}, u32[]{:S(2)}, u32[]{:S(2)}) collective-permute-start(f32[2,256,256]{2,1,0:T(8,128)} %pack.6), channel_id=1, source_target_pairs={{8,0},{16,8},{24,16},{32,24},{40,32},{48,40},{56,48},{64,56},{72,6... | collective-permute-start | bytes 1572872 | tf_op jit(solution)/shard_map/ppermute | solution.py:27
  30.2 73.9 %collective-permute-start.4 = (f32[2,256,128]{2,1,0:T(8,128)}, f32[2,256,128]{2,1,0:T(8,128)}, u32[]{:S(2)}, u32[]{:S(2)}) collective-permute-start(f32[2,256,128]{2,1,0:T(8,128)} %slice.103), channel_id=1, source_target_pairs={{0,1},{1,2},{2,3},{3,4},{4,5},{5,6},{6,7},{8,9},{9,10},{10,11},{11... | collective-permute-start | bytes 786440 | tf_op jit(solution)/shard_map/ppermute | solution.py:27
  35.2 21.5 %collective-permute-start.7 = (f32[2,256,256]{2,1,0:T(8,128)}, f32[2,256,256]{2,1,0:T(8,128)}, u32[]{:S(2)}, u32[]{:S(2)}) collective-permute-start(f32[2,256,256]{2,1,0:T(8,128)} %pack.7), channel_id=1, source_target_pairs={{8,0},{16,8},{24,16},{32,24},{40,32},{48,40},{56,48},{64,56},{72,6... | collective-permute-start | bytes 1572872 | tf_op jit(solution)/shard_map/ppermute | solution.py:27
  44.7 17.9 %collective-permute-start.8 = (f32[2,256,256]{2,1,0:T(8,128)}, f32[2,256,256]{2,1,0:T(8,128)S(1)}, u32[]{:S(2)}, u32[]{:S(2)}) collective-permute-start(f32[2,256,256]{2,1,0:T(8,128)} %pack.8), channel_id=1, source_target_pairs={{8,0},{16,8},{24,16},{32,24},{40,32},{48,40},{56,48},{64,56},{72,6... | collective-permute-start | bytes 1572872 | tf_op jit(solution)/shard_map/ppermute | solution.py:27
  48.9 7.8 %copy-start.22 = (bf16[8,256,256]{2,1,0:T(8,128)(2,1)S(1)}, bf16[8,256,256]{2,1,0:T(8,128)(2,1)}, u32[]{:S(2)}) copy-start(bf16[8,256,256]{2,1,0:T(8,128)(2,1)} %constant.45.clone.refs_7_) | copy-start | bytes 3145732
  64.9 47.1 %collective-permute-start.11 = (f32[2,256,256]{2,1,0:T(8,128)S(1)}, f32[2,256,256]{2,1,0:T(8,128)S(1)}, u32[]{:S(2)}, u32[]{:S(2)}) collective-permute-start(f32[2,256,256]{2,1,0:T(8,128)S(1)} %get-tuple-element.23.refs_2_), channel_id=1, source_target_pairs={{0,8},{8,16},{16,24},{24,32},{32,40},{40,48},{48,56},{56,64},{64,7... | collective-permute-start | bytes 1572872 | tf_op jit(solution)/shard_map/ppermute | solution.py:27
  68.4 43.6 %collective-permute-start.10 = (f32[2,256,256]{2,1,0:T(8,128)S(1)}, f32[2,256,256]{2,1,0:T(8,128)S(1)}, u32[]{:S(2)}, u32[]{:S(2)}) collective-permute-start(f32[2,256,256]{2,1,0:T(8,128)S(1)} %get-tuple-element.21.refs_1_), channel_id=1, source_target_pairs={{0,8},{8,16},{16,24},{24,32},{32,40},{40,48},{48,56},{56,64},{64,7... | collective-permute-start | bytes 1572872 | tf_op jit(solution)/shard_map/ppermute | solution.py:27
  82.0 30.0 %collective-permute-start.9 = (f32[2,256,256]{2,1,0:T(8,128)S(1)}, f32[2,256,256]{2,1,0:T(8,128)S(1)}, u32[]{:S(2)}, u32[]{:S(2)}) collective-permute-start(f32[2,256,256]{2,1,0:T(8,128)S(1)} %get-tuple-element.19.refs_0_), channel_id=1, source_target_pairs={{0,8},{8,16},{16,24},{24,32},{32,40},{40,48},{48,56},{56,64},{64,7... | collective-permute-start | bytes 1572872 | tf_op jit(solution)/shard_map/ppermute | solution.py:27
  83.9 5.0 %collective-permute-start.3 = (f32[2,8,1024]{2,1,0:T(8,128)S(1)}, f32[2,8,1024]{2,1,0:T(8,128)S(1)}, u32[]{:S(2)}, u32[]{:S(2)}) collective-permute-start(f32[2,8,1024]{2,1,0:T(8,128)S(1)} %get-tuple-element.40), channel_id=1, source_target_pairs={{8,0},{16,8},{24,16},{32,24},{40,32},{48,40},{56,48},{64,56},{72,6... | collective-permute-start | bytes 196616 | tf_op jit(solution)/shard_map/ppermute | solution.py:27
  88.9 15.2 %collective-permute-start.2 = (f32[2,8,1024]{2,1,0:T(8,128)S(1)}, f32[2,8,1024]{2,1,0:T(8,128)S(1)}, u32[]{:S(2)}, u32[]{:S(2)}) collective-permute-start(f32[2,8,1024]{2,1,0:T(8,128)S(1)} %get-tuple-element.41), channel_id=1, source_target_pairs={{0,8},{8,16},{16,24},{24,32},{32,40},{40,48},{48,56},{56,64},{64,7... | collective-permute-start | bytes 196616 | tf_op jit(solution)/shard_map/ppermute | solution.py:27
  107.5 15.4 %collective-permute-start.16 = (f32[3,256,256]{2,1,0:T(8,128)S(1)}, f32[3,256,256]{2,1,0:T(8,128)S(1)}, u32[]{:S(2)}, u32[]{:S(2)}) collective-permute-start(f32[3,256,256]{2,1,0:T(8,128)S(1)} %pad_maximum_fusion), channel_id=1, source_target_pairs={{1,0},{2,1},{3,2},{4,3},{5,4},{6,5},{7,6},{9,8},{10,9},{11,10},{12... | collective-permute-start | bytes 2359304 | tf_op jit(solution)/shard_map/ppermute | solution.py:27
  113.0 10.8 %copy-start.5 = (f32[5,2,256,256]{3,2,1,0:T(8,128)}, f32[5,2,256,256]{3,2,1,0:T(8,128)S(1)}, u32[]{:S(2)}) copy-start(f32[5,2,256,256]{3,2,1,0:T(8,128)S(1)} %gather.2.acc) | copy-start | bytes 7864324
  114.0 9.8 %collective-permute-start.12 = (f32[2,256,256]{2,1,0:T(8,128)S(1)}, f32[2,256,256]{2,1,0:T(8,128)S(1)}, u32[]{:S(2)}, u32[]{:S(2)}) collective-permute-start(f32[2,256,256]{2,1,0:T(8,128)S(1)} %get-tuple-element.37), channel_id=1, source_target_pairs={{0,1},{1,2},{2,3},{3,4},{4,5},{5,6},{6,7},{8,9},{9,10},{10,11},{11... | collective-permute-start | bytes 1572872 | tf_op jit(solution)/shard_map/ppermute | solution.py:27
  117.2 12.3 %collective-permute-start.17 = (f32[2,256,256]{2,1,0:T(8,128)}, f32[2,256,256]{2,1,0:T(8,128)}, u32[]{:S(2)}, u32[]{:S(2)}) collective-permute-start(f32[2,256,256]{2,1,0:T(8,128)} %get-tuple-element.36), channel_id=1, source_target_pairs={{1,0},{2,1},{3,2},{4,3},{5,4},{6,5},{7,6},{9,8},{10,9},{11,10},{12... | collective-permute-start | bytes 1572872 | tf_op jit(solution)/shard_map/ppermute | solution.py:27
  134.7 87.9 %collective-permute-start.18 = (f32[2,256,256]{2,1,0:T(8,128)}, f32[2,256,256]{2,1,0:T(8,128)}, u32[]{:S(2)}, u32[]{:S(2)}) collective-permute-start(f32[2,256,256]{2,1,0:T(8,128)} %pack.9), channel_id=1, source_target_pairs={{8,0},{16,8},{24,16},{32,24},{40,32},{48,40},{56,48},{64,56},{72,6... | collective-permute-start | bytes 1572872 | tf_op jit(solution)/shard_map/ppermute | solution.py:27
  136.0 8.1 %copy-start.10 = (f32[4,2,256,256]{3,2,1,0:T(8,128)S(1)}, f32[4,2,256,256]{3,2,1,0:T(8,128)}, u32[]{:S(2)}) copy-start(f32[4,2,256,256]{3,2,1,0:T(8,128)} %refs_6_.5) | copy-start | bytes 6291460
  139.0 94.8 %collective-permute-start.19 = (f32[2,256,256]{2,1,0:T(8,128)}, f32[2,256,256]{2,1,0:T(8,128)}, u32[]{:S(2)}, u32[]{:S(2)}) collective-permute-start(f32[2,256,256]{2,1,0:T(8,128)} %pack.10), channel_id=1, source_target_pairs={{8,0},{16,8},{24,16},{32,24},{40,32},{48,40},{56,48},{64,56},{72,6... | collective-permute-start | bytes 1572872 | tf_op jit(solution)/shard_map/ppermute | solution.py:27
  221.2 15.5 %collective-permute-start.20 = (f32[2,256,256]{2,1,0:T(8,128)}, f32[2,256,256]{2,1,0:T(8,128)S(1)}, u32[]{:S(2)}, u32[]{:S(2)}) collective-permute-start(f32[2,256,256]{2,1,0:T(8,128)} %pack.11), channel_id=1, source_target_pairs={{8,0},{16,8},{24,16},{32,24},{40,32},{48,40},{56,48},{64,56},{72,6... | collective-permute-start | bytes 1572872 | tf_op jit(solution)/shard_map/ppermute | solution.py:27
  225.4 8.5 %copy-start.24 = (bf16[8,256,256]{2,1,0:T(8,128)(2,1)S(1)}, bf16[8,256,256]{2,1,0:T(8,128)(2,1)}, u32[]{:S(2)}) copy-start(bf16[8,256,256]{2,1,0:T(8,128)(2,1)} %constant.45.clone.refs_7_) | copy-start | bytes 3145732
  237.7 21.3 %collective-permute-start.23 = (f32[2,256,256]{2,1,0:T(8,128)S(1)}, f32[2,256,256]{2,1,0:T(8,128)S(1)}, u32[]{:S(2)}, u32[]{:S(2)}) collective-permute-start(f32[2,256,256]{2,1,0:T(8,128)S(1)} %get-tuple-element.31.refs_2_), channel_id=1, source_target_pairs={{0,8},{8,16},{16,24},{24,32},{32,40},{40,48},{48,56},{56,64},{64,7... | collective-permute-start | bytes 1572872 | tf_op jit(solution)/shard_map/ppermute | solution.py:27
  240.7 27.1 %collective-permute-start.22 = (f32[2,256,256]{2,1,0:T(8,128)S(1)}, f32[2,256,256]{2,1,0:T(8,128)S(1)}, u32[]{:S(2)}, u32[]{:S(2)}) collective-permute-start(f32[2,256,256]{2,1,0:T(8,128)S(1)} %get-tuple-element.29.refs_1_), channel_id=1, source_target_pairs={{0,8},{8,16},{16,24},{24,32},{32,40},{40,48},{48,56},{56,64},{64,7... | collective-permute-start | bytes 1572872 | tf_op jit(solution)/shard_map/ppermute | solution.py:27
  256.0 18.8 %collective-permute-start.21 = (f32[2,256,256]{2,1,0:T(8,128)S(1)}, f32[2,256,256]{2,1,0:T(8,128)S(1)}, u32[]{:S(2)}, u32[]{:S(2)}) collective-permute-start(f32[2,256,256]{2,1,0:T(8,128)S(1)} %get-tuple-element.27.refs_0_), channel_id=1, source_target_pairs={{0,8},{8,16},{16,24},{24,32},{32,40},{40,48},{48,56},{56,64},{64,7... | collective-permute-start | bytes 1572872 | tf_op jit(solution)/shard_map/ppermute | solution.py:27
  274.8 13.8 %copy-start.4 = (f32[8,256,256]{2,1,0:T(8,128)S(1)}, f32[8,256,256]{2,1,0:T(8,128)}, u32[]{:S(2)}) copy-start(f32[8,256,256]{2,1,0:T(8,128)} %copy-done.2) | copy-start | bytes 6291460
  277.4 72.0 %collective-permute-start.24 = (f32[2,256,256]{2,1,0:T(8,128)S(1)}, f32[2,256,256]{2,1,0:T(8,128)S(1)}, u32[]{:S(2)}, u32[]{:S(2)}) collective-permute-start(f32[2,256,256]{2,1,0:T(8,128)S(1)} %slice_bitcast_fusion.2), channel_id=1, source_target_pairs={{0,1},{1,2},{2,3},{3,4},{4,5},{5,6},{6,7},{8,9},{9,10},{10,11},{11... | collective-permute-start | bytes 1572872 | tf_op jit(solution)/shard_map/ppermute | solution.py:27
  279.3 9.3 %collective-permute-start.15 = (f32[2,256,128]{2,1,0:T(8,128)S(1)}, f32[2,256,128]{2,1,0:T(8,128)S(1)}, u32[]{:S(2)}, u32[]{:S(2)}) collective-permute-start(f32[2,256,128]{2,1,0:T(8,128)S(1)} %slice.142), channel_id=1, source_target_pairs={{0,1},{1,2},{2,3},{3,4},{4,5},{5,6},{6,7},{8,9},{9,10},{10,11},{11... | collective-permute-start | bytes 786440 | tf_op jit(solution)/shard_map/ppermute | solution.py:27
  281.3 6.1 %collective-permute-start.14 = (f32[2,8,1024]{2,1,0:T(8,128)S(1)}, f32[2,8,1024]{2,1,0:T(8,128)S(1)}, u32[]{:S(2)}, u32[]{:S(2)}) collective-permute-start(f32[2,8,1024]{2,1,0:T(8,128)S(1)} %get-tuple-element.38), channel_id=1, source_target_pairs={{8,0},{16,8},{24,16},{32,24},{40,32},{48,40},{56,48},{64,56},{72,6... | collective-permute-start | bytes 196616 | tf_op jit(solution)/shard_map/ppermute | solution.py:27
  282.6 6.0 %collective-permute-start.13 = (f32[2,8,1024]{2,1,0:T(8,128)S(1)}, f32[2,8,1024]{2,1,0:T(8,128)S(1)}, u32[]{:S(2)}, u32[]{:S(2)}) collective-permute-start(f32[2,8,1024]{2,1,0:T(8,128)S(1)} %get-tuple-element.39), channel_id=1, source_target_pairs={{0,8},{8,16},{16,24},{24,32},{32,40},{40,48},{48,56},{56,64},{64,7... | collective-permute-start | bytes 196616 | tf_op jit(solution)/shard_map/ppermute | solution.py:27
  291.5 40.6 %copy-start.16 = (f32[2,256,1024]{2,1,0:T(8,128)}, f32[2,256,1024]{2,1,0:T(8,128)S(1)}, u32[]{:S(2)}) copy-start(f32[2,256,1024]{2,1,0:T(8,128)S(1)} %get-tuple-element.26.base) | copy-start | bytes 6291460
  291.5 40.6 %copy-start.18 = (f32[4,256,256]{2,1,0:T(8,128)}, f32[4,256,256]{2,1,0:T(8,128)S(1)}, u32[]{:S(2)}) copy-start(f32[4,256,256]{2,1,0:T(8,128)S(1)} %get-tuple-element.32.weight) | copy-start | bytes 3145732
  (22 other events, 65.8 us)

commit v3 on v0

v3 whole, which is shorter than its diff:
```python
import functools
import math

import jax
import jax.numpy as jnp
import ml_dtypes
import numpy as np
from jax import lax
from jax.experimental import pallas as pl
from jax.experimental.pallas import tpu as pltpu
from jax.sharding import PartitionSpec as P

step_object = 1.0
step_probe = 1.0
smoothing = 0.05
object_floor = 1.0
probe_floor = 0.001
SIDE = 256
HALF = 128
MODES = 4
VMEM = pltpu.VMEM
f32 = jnp.float32


def shifted(value, axis, steps):
    count = lax.axis_size(axis)
    leading, last = (max(0, -steps), min(count, count - steps))
    return lax.ppermute(value, axis, [(source, source + steps) for source in range(leading, last)])


def matrices():
    k, n = np.arange(HALF)[:, None], np.arange(HALF)[None, :]
    out = []
    for odd in (0, 1):
        angle = -2.0 * np.pi * (((2 * k + odd) * n) % SIDE) / SIDE
        re, im = np.cos(angle) / math.sqrt(SIDE), np.sin(angle) / math.sqrt(SIDE)
        big = np.block([[re, -im], [im, re]])
        for matrix in (big, big.T):
            high = matrix.astype(ml_dtypes.bfloat16)
            low = (matrix - high.astype(np.float64)).astype(ml_dtypes.bfloat16)
            out += [high, low]
    return np.stack(out)


def split(value):
    high = value.astype(jnp.bfloat16)
    return high, (value - high.astype(f32)).astype(jnp.bfloat16)


def dot(a, b):
    return jnp.dot(a, b, preferred_element_type=f32)


def left(mats, index, value):
    high, low = split(value)
    a, b = mats[index], mats[index + 1]
    return dot(a, high) + dot(b, high) + dot(a, low)


def right(value, mats, index):
    high, low = split(value)
    a, b = mats[index], mats[index + 1]
    return dot(high, a) + dot(high, b) + dot(low, a)


def cat(axis, *values):
    return jnp.concatenate(values, axis=axis)


def iotas():
    shape = (SIDE, SIDE)
    return lax.broadcasted_iota(jnp.int32, shape, 0), lax.broadcasted_iota(jnp.int32, shape, 1)


def roll2(value, rows, cols):
    return pltpu.roll(pltpu.roll(value, rows, 0), cols, 1)


MESH = pl.DeviceIdType.MESH
PLANES = 2 * MODES + 1


def at(base, index, size):
    return pl.ds(pl.multiple_of(base + index * size, 8), size)


class Links:
    def __init__(self, send, recv):
        self.send, self.recv, self.used = send, recv, 0

    def copy(self, src, dst, device_id):
        i = self.used
        self.used += 1
        made = pltpu.make_async_remote_copy(
            src_ref=src,
            dst_ref=dst,
            send_sem=self.send.at[i],
            recv_sem=self.recv.at[i],
            device_id=device_id,
            device_id_type=MESH,
        )
        made.start()
        return made


def whole_kernel(
    batches, slots, chunks, mesh_rows, mesh_cols,
    info, tile, probe_in, pats_in, mats, perm, out_tile, out_probe,
    ext, probe, raw, pats, rolled, arrived, grads, gained, acc, base, weight, side, from_left, from_right,
    above, below, before, psi, pg, got1, half, got2, got3, got4, send, recv, slot_send, slot_recv, local,
):
    row, col = lax.axis_index("row"), lax.axis_index("col")
    y, x, z, core = lax.div(row, 4), lax.rem(row, 4), lax.div(col, 2), lax.rem(col, 2)
    first, second = y + core * (z - y), z + core * (y - z)
    device = lambda y, x, z, core: (y * 4 + x, z * 2 + core)
    sibling = device(y, x, z, 1 - core)
    turn = lambda value, step: lax.rem(value + step, 4)
    along_first = lambda j: device(turn(y, j * (1 - core)), x, turn(z, j * core), core)
    along_second = lambda j: device(turn(y, j * core), x, turn(z, j * (1 - core)), core)
    along_x = lambda j: device(y, turn(x, j), z, core)
    up = (lax.rem(row + mesh_rows - 1, mesh_rows), col)
    down = (lax.rem(row + 1, mesh_rows), col)
    before_me = (row, lax.rem(col + mesh_cols - 1, mesh_cols))
    after_me = (row, lax.rem(col + 1, mesh_cols))
    links = Links(send, recv)

    loads = [
        pltpu.make_async_copy(tile.at[:, :, pl.ds(j * SIDE, SIDE)], ext.at[j], local.at[j])
        for j in range(chunks)
    ]
    loads.append(pltpu.make_async_copy(pats_in, raw, local.at[chunks]))
    loads.append(pltpu.make_async_copy(probe_in, probe.at[0], local.at[chunks + 1]))
    for load in loads:
        load.start()
    barrier = pltpu.get_barrier_semaphore()
    peers = [sibling, up, down, before_me, after_me]
    peers += [f(j) for f in (along_first, along_second, along_x) for j in (1, 2, 3)]
    for peer in peers:
        pl.semaphore_signal(barrier, inc=1, device_id=peer, device_id_type=MESH)
    pl.semaphore_wait(barrier, len(peers))

    rows, cols = iotas()
    rim = links.copy(tile.at[:, :, pl.ds(0, SIDE)], ext.at[chunks], before_me)
    sent = [rim]

    def where_to(b, who, s, rows_below):
        k, r, cm, live = [info[b, who, s, j] for j in range(4)]
        inside = (rows < r) if rows_below else (rows >= r)
        return jnp.where(inside & (live == 1), k + (cols < cm).astype(jnp.int32), -1)

    def start_halos(b):
        return [
            links.copy(ext.at[pl.ds(0, chunks), :, pl.ds(SIDE - 8, 8), :], above.at[b], down),
            links.copy(ext.at[pl.ds(0, chunks), :, pl.ds(0, 8), :], below.at[b], up),
            links.copy(ext.at[chunks - 1, :, :, pl.ds(HALF, HALF)], before.at[b], after_me),
        ]

    def slot_copy(b, s, kind):
        src, dst, peer = (rolled, arrived, up) if kind == 0 else (grads, gained, down)
        i = (2 * b + kind) * slots + s
        return pltpu.make_async_remote_copy(
            src_ref=src.at[s],
            dst_ref=dst.at[b, s],
            send_sem=slot_send.at[i],
            recv_sem=slot_recv.at[i],
            device_id=peer,
            device_id_type=MESH,
        )

    def start_rims(b):
        def one(s, carry):
            k, cm = info[b, 1, s, 0], info[b, 1, s, 2]
            for part in range(2):
                rolled[s, part] = jnp.where(cols >= cm, ext[k, part], ext[k + 1, part])
            slot_copy(b, s, 0).start()
            return carry

        lax.fori_loop(0, slots, one, 0)

    def order_patterns():
        def one(i, carry):
            high, low = split(raw[i])
            value = dot(perm[0], high) + dot(perm[0], low)
            high, low = split(value)
            pats[i] = dot(high, perm[1]) + dot(low, perm[1])
            return carry

        lax.fori_loop(0, batches * slots, one, 0)

    def prepare(b, halos):
        power = probe[b, 0] * probe[b, 0]
        for plane in range(1, 2 * MODES):
            power = power + probe[b, plane] * probe[b, plane]
        pg[2 * MODES] = power
        weight[...] = jnp.zeros_like(weight)

        def one(s, carry):
            for who in range(4):
                value = roll2(pg[2 * MODES], info[b, who, s, 1], info[b, who, s, 2])
                chunk = where_to(b, who, s, who % 2 == 1)
                if who < 2:
                    for j in range(chunks):
                        weight[j] += jnp.where(chunk == j, value, 0.0)
                else:
                    weight[0] += jnp.where(chunk == chunks, value, 0.0)
            return carry

        lax.fori_loop(0, slots, one, 0)
        for copy in halos:
            copy.wait_recv()
        for part in range(2):
            for j in range(chunks):
                here = ext[j, part]
                top = jnp.where(row > 0, above[b, j, part, 7:8, :], 0.0)
                bottom = jnp.where(row < mesh_rows - 1, below[b, j, part, 0:1, :], 0.0)
                if j > 0:
                    lhs = ext[j - 1, part, :, HALF:][:, HALF - 1 : HALF]
                else:
                    lhs = jnp.where(col > 0, before[b, part, :, HALF - 1 : HALF], 0.0)
                rhs = ext[j + 1, part, :, :HALF][:, 0:1]
                if j == chunks - 1:
                    rhs = jnp.where(col < mesh_cols - 1, rhs, 0.0)
                neighbours = jnp.where(rows == 0, top, pltpu.roll(here, 1, 0))
                neighbours += jnp.where(rows == SIDE - 1, bottom, pltpu.roll(here, SIDE - 1, 0))
                neighbours += jnp.where(cols == 0, lhs, pltpu.roll(here, 1, 1))
                neighbours += jnp.where(cols == SIDE - 1, rhs, pltpu.roll(here, SIDE - 1, 1))
                base[j, part] = here + (step_object * smoothing) * (neighbours - 4.0 * here)
        if b + 1 < batches:
            copies = [
                links.copy(base.at[0], side.at[pl.ds(0, 2)], before_me),
                links.copy(weight.at[0], side.at[2], before_me),
            ]
            sent.extend(copies)
            return copies
        return []

    def run_slots(b):
        pg[...] = jnp.zeros_like(pg)

        def one(s, carry):
            slot_copy(b, s, 0).wait_recv()
            k, r, cm, live = [info[b, 0, s, j] for j in range(4)]
            alive = live.astype(f32)
            window = []
            for part in range(2):
                own = jnp.where(cols >= cm, ext[k, part], ext[k + 1, part])
                value = jnp.where(rows >= r, own, arrived[b, s, part])
                window.append(roll2(value, lax.rem(SIDE - r, SIDE), lax.rem(SIDE - cm, SIDE)))
            xr, xi = window
            total_e = total_o = None
            for m in range(MODES):
                pr, pi = probe[b, 2 * m], probe[b, 2 * m + 1]
                wr, wi = pr * xr - pi * xi, pr * xi + pi * xr
                even = left(mats, 0, cat(0, wr[:HALF] + wr[HALF:], wi[:HALF] + wi[HALF:]))
                odd = left(mats, 4, cat(0, wr[:HALF] - wr[HALF:], wi[:HALF] - wi[HALF:]))
                tr, ti = cat(0, even[:HALF], odd[:HALF]), cat(0, even[HALF:], odd[HALF:])
                pe = right(cat(1, tr[:, :HALF] + tr[:, HALF:], ti[:, :HALF] + ti[:, HALF:]), mats, 2)
                po = right(cat(1, tr[:, :HALF] - tr[:, HALF:], ti[:, :HALF] - ti[:, HALF:]), mats, 6)
                psi[m, 0], psi[m, 1] = pe, po
                total_e = pe * pe if m == 0 else total_e + pe * pe
                total_o = po * po if m == 0 else total_o + po * po
            pattern = pats[b * slots + s]
            de = (total_e[:, :HALF] + total_e[:, HALF:] - pattern[:, :HALF]) * alive
            do = (total_o[:, :HALF] + total_o[:, HALF:] - pattern[:, HALF:]) * alive
            de, do = cat(1, de, de), cat(1, do, do)
            grad_r = grad_i = None
            for m in range(MODES):
                ue, uo = right(psi[m, 0] * de, mats, 0), right(psi[m, 1] * do, mats, 4)
                plus, minus = ue + uo, ue - uo
                tr, ti = cat(1, plus[:, :HALF], minus[:, :HALF]), cat(1, plus[:, HALF:], minus[:, HALF:])
                ze = left(mats, 2, cat(0, tr[:HALF], ti[:HALF]))
                zo = left(mats, 6, cat(0, tr[HALF:], ti[HALF:]))
                plus, minus = ze + zo, ze - zo
                br, bi = cat(0, plus[:HALF], minus[:HALF]), cat(0, plus[HALF:], minus[HALF:])
                pr, pi = probe[b, 2 * m], probe[b, 2 * m + 1]
                gr, gi = pr * br + pi * bi, pr * bi - pi * br
                grad_r = gr if m == 0 else grad_r + gr
                grad_i = gi if m == 0 else grad_i + gi
                pg[2 * m] += xr * br + xi * bi
                pg[2 * m + 1] += xr * bi - xi * br
            pg[2 * MODES] += (xr * xr + xi * xi) * alive
            grads[s, 0] = roll2(grad_r, r, cm)
            grads[s, 1] = roll2(grad_i, r, cm)
            slot_copy(b, s, 1).start()
            return carry

        lax.fori_loop(0, slots, one, 0)

    def gather(b, s):
        slot_copy(b, s, 1).wait_recv()
        own, theirs = where_to(b, 0, s, False), where_to(b, 1, s, True)
        for part in range(2):
            for j in range(chunks + 1):
                value = jnp.where(own == j, grads[s, part], 0.0) + jnp.where(theirs == j, gained[b, s, part], 0.0)
                if s == 0:
                    acc[j, part] = value
                else:
                    acc[j, part] += value

    order = (2, 1, 3, 0)

    def reduce_cores():
        ones = []
        for step in order:
            theirs, there = at((1 - core) * HALF, turn(second, step), 32), at(0, turn(second, step), 32)
            ones.append(links.copy(pg.at[:, theirs, :], got1.at[:, there, :], sibling))
        sent.extend(ones)
        return ones

    def reduce_first(ones):
        twos = []
        for i, step in enumerate(order):
            piece = turn(first, step)
            ones[i].wait_recv()
            mine, there = at(core * HALF, piece, 32), at(0, piece, 32)
            half[:, there, :] = pg[:, mine, :] + got1[:, there, :]
            if step:
                twos.append(links.copy(half.at[:, there, :], got2.at[step - 1], along_first(step)))
        sent.extend(twos)
        return twos

    def reduce_second(twos):
        threes = []
        for copy in twos:
            copy.wait_recv()
        for step in order:
            piece = turn(second, step)
            there, within = at(first * 32, piece, 8), at(0, piece, 8)
            value = half[:, there, :] + got2[0, :, within, :]
            half[:, there, :] = value + got2[1, :, within, :] + got2[2, :, within, :]
            if step:
                threes.append(links.copy(half.at[:, there, :], got3.at[step - 1], along_second(step)))
        sent.extend(threes)
        return threes

    def reduce_x(threes):
        fours = []
        for copy in threes:
            copy.wait_recv()
        there = at(first * 32, second, 8)
        got4[x] = half[:, there, :] + got3[0] + got3[1] + got3[2]
        for step in (2, 1, 3):
            fours.append(links.copy(got4.at[x], got4.at[x], along_x(step)))
        sent.extend(fours)
        return fours

    def spread_second(b, fours):
        for copy in fours:
            copy.wait_recv()
        total = got4[0] + got4[1] + got4[2] + got4[3]
        scale = step_probe / (total[2 * MODES] + probe_floor)
        mine = at(core * HALF + first * 32, second, 8)
        new = probe.at[b + 1]
        for plane in range(2 * MODES):
            new[plane, mine, :] = probe[b, plane, mine, :] - scale * total[plane]
        block = new.at[:, mine, :]
        copies = [links.copy(block, block, along_second(step)) for step in (2, 1, 3)]
        sent.extend(copies)
        return copies

    def spread_first(b, copies):
        for copy in copies:
            copy.wait_recv()
        block = probe.at[b + 1, :, at(core * HALF, first, 32), :]
        twos = [links.copy(block, block, along_first(step)) for step in (2, 1, 3)]
        threes = [links.copy(block, block, sibling)]
        sent.extend(twos + threes)
        return twos, threes

    def spread_cores(b, twos, threes):
        for i, step in ((1, 1), (2, 3), (0, 2)):
            twos[i].wait_recv()
            block = probe.at[b + 1, :, at(core * HALF, turn(first, 4 - step), 32), :]
            copy = links.copy(block, block, sibling)
            threes.append(copy)
            sent.append(copy)
        for copy in threes:
            copy.wait_recv()

    for load in loads[:chunks]:
        load.wait()
    halos = start_halos(0)
    for load in loads[chunks:]:
        load.wait()
    order_patterns()
    rim.wait_recv()
    start_rims(0)
    got1s, got2s, got3s, got4s = got1, got2, got3, got4
    stores = []
    for b in range(batches):
        more = b + 1 < batches
        got1, got2, got3, got4 = got1s.at[b], got2s.at[b], got3s.at[b], got4s.at[b]
        sides = prepare(b, halos)
        run_slots(b)
        ones = reduce_cores()
        for s in range(slots - 1):
            gather(b, s)
        twos = reduce_first(ones)
        gather(b, slots - 1)
        to_right = links.copy(acc.at[chunks], from_left.at[b], after_me)
        sent.append(to_right)
        if more:
            to_left = links.copy(acc.at[0], from_right, before_me)
            sent.append(to_left)
        threes = reduce_second(twos)
        fours = reduce_x(threes)
        if not more:
            spread = spread_second(b, fours)
        for copy in halos:
            copy.wait_send()
        for j in list(range(1, chunks)) + [0]:
            if j == 0:
                to_right.wait_recv()
            scale = step_object / (weight[j] + object_floor)
            for part in range(2):
                value = acc[j, part] + from_left[b, part] if j == 0 else acc[j, part]
                ext[j, part] = base[j, part] - scale * value
            if not more:
                store = pltpu.make_async_copy(ext.at[j], out_tile.at[:, :, pl.ds(j * SIDE, SIDE)], local.at[j])
                store.start()
                stores.append(store)
        for s in range(slots):
            slot_copy(b, s, 0).wait_send()
            slot_copy(b, s, 1).wait_send()
        if more:
            to_left.wait_recv()
            for copy in sides:
                copy.wait_recv()
            scale = step_object / (side[2] + object_floor)
            for part in range(2):
                ext[chunks, part] = side[part] - scale * (acc[chunks, part] + from_right[part])
            start_rims(b + 1)
            halos = start_halos(b + 1)
            spread = spread_second(b, fours)
        twos, threes = spread_first(b, spread)
        spread_cores(b, twos, threes)
        if more:
            for copy in sent:
                copy.wait_send()
            sent.clear()
    last = pltpu.make_async_copy(probe.at[batches], out_probe, local.at[chunks + 1])
    last.start()
    for copy in sent:
        copy.wait_send()
    for store in stores + [last]:
        store.wait()


def shards(object_field, probe_modes, offsets, live_counts, patterns):
    tile_rows, tile_cols = object_field.shape[1:]
    chunks = tile_cols // SIDE
    batches, slots = offsets.shape[:2]
    mesh_rows, mesh_cols = lax.axis_size("row"), lax.axis_size("col")
    anchor = jnp.stack([lax.axis_index("row") * tile_rows, lax.axis_index("col") * tile_cols])
    local = offsets - anchor[None, None, :]
    row_at, col_at = local[..., 0], local[..., 1]
    live = (jnp.arange(slots)[None, :] < live_counts).astype(jnp.int32)
    own = jnp.stack([col_at // SIDE, row_at, col_at % SIDE, live], axis=-1)
    two = jnp.stack([own, shifted(own, "row", 1)], axis=1)
    info = jnp.concatenate([two, shifted(two, "col", 1)], axis=1)
    perm = np.zeros((SIDE, SIDE), np.float32)
    j = np.arange(SIDE)
    perm[j, (j % 2) * HALF + j // 2] = 1.0
    perm = jnp.asarray(np.stack([perm.T, perm]), jnp.bfloat16)

    vmem, hbm = pl.BlockSpec(memory_space=VMEM), pl.BlockSpec(memory_space=pl.ANY)
    block = (2, SIDE, SIDE)
    buf = lambda *shape: pltpu.VMEM(shape, f32)
    dma = pltpu.SemaphoreType.DMA
    tile, probe = pl.pallas_call(
        functools.partial(whole_kernel, batches, slots, chunks, mesh_rows, mesh_cols),
        in_specs=[pl.BlockSpec(memory_space=pltpu.SMEM), hbm, hbm, hbm, vmem, vmem],
        out_specs=[hbm, hbm],
        out_shape=[
            jax.ShapeDtypeStruct(object_field.shape, f32),
            jax.ShapeDtypeStruct((2 * MODES, SIDE, SIDE), f32),
        ],
        scratch_shapes=[
            buf(chunks + 1, *block),
            buf(batches + 1, 2 * MODES, SIDE, SIDE),
            buf(batches * slots, SIDE, SIDE),
            buf(batches * slots, SIDE, SIDE),
            buf(slots, *block),
            buf(batches, slots, *block),
            buf(slots, *block),
            buf(batches, slots, *block),
            buf(chunks + 1, *block),
            buf(chunks, *block),
            buf(chunks, SIDE, SIDE),
            buf(3, SIDE, SIDE),
            buf(batches, *block),
            buf(*block),
            buf(batches, chunks, 2, 8, SIDE),
            buf(batches, chunks, 2, 8, SIDE),
            buf(batches, 2, SIDE, HALF),
            buf(MODES, *block),
            buf(PLANES, SIDE, SIDE),
            buf(batches, PLANES, HALF, SIDE),
            buf(PLANES, HALF, SIDE),
            buf(batches, 3, PLANES, 32, SIDE),
            buf(batches, 3, PLANES, 8, SIDE),
            buf(batches, 4, PLANES, 8, SIDE),
            dma((80,)),
            dma((80,)),
            dma((2 * batches * slots,)),
            dma((2 * batches * slots,)),
            dma((chunks + 2,)),
        ],
        compiler_params=pltpu.CompilerParams(
            collective_id=0, has_side_effects=True, vmem_limit_bytes=60 * 2**20
        ),
        name="reconstruct",
    )(
        info,
        object_field,
        probe_modes.reshape(2 * MODES, SIDE, SIDE),
        patterns.reshape(batches * slots, SIDE, SIDE),
        jnp.asarray(matrices()),
        perm,
    )
    return (tile, probe.reshape(probe_modes.shape))


def solution(mesh):
    placed = (
        P(None, "row", "col"),
        P(),
        P(None, ("row", "col"), None),
        P(None, ("row", "col")),
        P(None, ("row", "col"), None, None),
    )
    return jax.shard_map(
        shards, mesh=mesh, in_specs=placed, out_specs=(P(None, "row", "col"), P()), check_vma=False
    )
```

time: 1090 us -> 236 us (0.22)
  waiting for transfers between devices: 553 us -> 1.41 us
  starting transfers between devices: 261 us -> 8.89 us
  Pallas kernels: 0 us -> 215 us
  matrix products: 89.7 us -> 0 us
  local copies, waits for them, and re-layouts: 89.3 us -> 4.83 us
  other arithmetic: 45.1 us -> 2.2 us
  loops' own time: 26.4 us -> 0 us
  between operations: 14.7 us -> 0.68 us
    psum x2 -> x0, waiting for transfers between devices: 341 us -> none  [one_batch(): lax.psum((probe_total, power_total), ('row', 'col'))]
    ppermute x8 -> x2, starting transfers between devices: 238 us -> 8.89 us  [shifted(): lax.ppermute(value, axis, [(source, source + steps) for source in range(l...]
    pallas_call x0 -> x1, Pallas kernels: none -> 215 us  [shards(): pl.pallas_call(functools.partial(whole_kernel, batches, slots, chunks, me...]
    ppermute x8 -> x2, waiting for transfers between devices: 208 us -> 1.41 us  [shifted(): lax.ppermute(value, axis, [(source, source + steps) for source in range(l...]
    dot_general x32 -> x0, matrix products: 89.7 us -> none  [the longest x16 45.9 us: apply_columns(): return jnp.einsum('mjk,kl->mjl', values, matrix, precision=highest)]
    another operation x6 -> x0, loops' own time: 26.4 us -> none  [the longest x2 16.1 us: run_items(): return lax.fori_loop(first_item, last_item, visit_item, start_state)]
    gather x18 -> x0, local copies, waits for them, and re-layouts: 24.3 us -> none
    ppermute x8 -> x0, starting transfers between devices: 22.9 us -> none  [the longest x4 15.1 us: padded(): before = lax.ppermute(last, axis, up)]
  transfers between devices with their start and end apart: 18 -> 2, of which waited for: 12 -> 2; matrix products, arithmetic and copies ran while one was open for 2% -> 0% of each run, Pallas kernels for 0% -> 0%
where the time goes in v3:
time: 236 us; the launch traced here: 233 us
  Pallas kernels  215 us (91%)
  starting transfers between devices  8.89 us (4%)
  local copies, waits for them, and re-layouts  4.83 us (2%)
    pallas_call x1, Pallas kernels, shards(): pl.pallas_call(functools.partial(whole_kernel, batches, slots, chunks, me...  215 us
    ppermute x2, starting transfers between devices, shifted(): lax.ppermute(value, axis, [(source, source + steps) for source in range(l...  8.89 us
  transfers between devices with their start and end apart: 2, of which 2 were waited for; matrix products, arithmetic and copies ran while one was open for 0% of the time, Pallas kernels for 0%

profile of v3, /device:TPU:1, one launch (start us, length us, event | category | flops | bytes accessed | tf_op | source)
XLA Modules:
  0.0 232.7 jit_solution(7750311412811138461)
XLA Ops:
  0.6 0.7 compare_convert_fusion
  1.4 0.1 pad_add_fusion.3
  1.4 0.8 broadcast_subtract_fusion
  2.2 3.9 %collective-permute-start = (s32[2,3,4]{1,2,0:T(4,128)S(1)}, s32[2,3,4]{1,2,0:T(4,128)S(1)}, u32[]{:S(2)}, u32[]{:S(2)}) collective-permute-start(s32[2,3,4]{1,2,0:T(4,128)S(1)} %get-tuple-element.9), channel_id=1, source_target_pairs={{0,8},{8,16},{16,24},{24,32},{32,40},{40,48},{48,56},{56,64},{64,7... | collective-permute-start | bytes 296 | tf_op jit(solution)/shard_map/ppermute | solution.py:28
  6.2 0.1 copy.13
  6.3 0.6 collective-permute-done
  6.9 0.1 copy.14
  7.0 4.9 %collective-permute-start.1 = (s32[2,2,3,4]{3,2,1,0:T(4,128)S(1)}, s32[2,2,3,4]{3,2,1,0:T(4,128)S(1)}, u32[]{:S(2)}, u32[]{:S(2)}) collective-permute-start(s32[2,2,3,4]{3,2,1,0:T(4,128)S(1)} %pad_add_fusion.1), channel_id=1, source_target_pairs={{0,1},{1,2},{2,3},{3,4},{4,5},{5,6},{6,7},{8,9},{9,10},{10,11},{11... | collective-permute-start | bytes 584 | tf_op jit(solution)/shard_map/ppermute | solution.py:28
  12.0 0.8 collective-permute-done.1
  12.8 0.6 pad_add_fusion.info
  13.4 214.7 %reconstruct.1 = (f32[2,256,1024]{2,1,0:T(8,128)}, f32[8,256,256]{2,1,0:T(8,128)}) custom-call(s32[2,4,3,4]{3,2,1,0:T(4,128)} %pad_add_fusion.info, f32[2,256,1024]{2,1,0:T(8,128)} %tile.1, f32[8,256,256]{2,1,0:T(8,128)} %bitcast.9, f32[6,256,256]{2,1,0:T(8,128)} %bitcast.11, bf16[8,256,256]{2,1,0:T(8,128)(2,1)} %constant.44.clone.mats, ...), custom_call_target="tpu_custom_call" | custom-call | tf_op jit(solution)/shard_map/reconstruct/pallas_call | solution.py:470
  228.1 0.0 copy-start
  228.1 3.3 %copy.21 = f32[2,256,1024]{2,1,0:T(8,128)} copy(f32[2,256,1024]{2,1,0:T(8,128)} %get-tuple-element.13) | data formatting | bytes 4194304
  231.4 0.0 copy-done
  231.4 1.3 copy.22
  (4 shorter events, 0.0 us)
Async XLA Ops:
  2.2 4.7 %collective-permute-start = (s32[2,3,4]{1,2,0:T(4,128)S(1)}, s32[2,3,4]{1,2,0:T(4,128)S(1)}, u32[]{:S(2)}, u32[]{:S(2)}) collective-permute-start(s32[2,3,4]{1,2,0:T(4,128)S(1)} %get-tuple-element.9), channel_id=1, source_target_pairs={{0,8},{8,16},{16,24},{24,32},{32,40},{40,48},{48,56},{56,64},{64,7... | collective-permute-start | bytes 296 | tf_op jit(solution)/shard_map/ppermute | solution.py:28
  7.0 5.7 %collective-permute-start.1 = (s32[2,2,3,4]{3,2,1,0:T(4,128)S(1)}, s32[2,2,3,4]{3,2,1,0:T(4,128)S(1)}, u32[]{:S(2)}, u32[]{:S(2)}) collective-permute-start(s32[2,2,3,4]{3,2,1,0:T(4,128)S(1)} %pad_add_fusion.1), channel_id=1, source_target_pairs={{0,1},{1,2},{2,3},{3,4},{4,5},{5,6},{6,7},{8,9},{9,10},{10,11},{11... | collective-permute-start | bytes 584 | tf_op jit(solution)/shard_map/ppermute | solution.py:28
  228.1 3.3 %copy-start = (f32[8,256,256]{2,1,0:T(8,128)S(1)}, f32[8,256,256]{2,1,0:T(8,128)}, u32[]{:S(2)}) copy-start(f32[8,256,256]{2,1,0:T(8,128)} %get-tuple-element.5) | copy-start | bytes 6291460

commit v4 on v3

--- a/solution.py
+++ b/solution.py
@@ -20,12 +20,6 @@
 MODES = 4
 VMEM = pltpu.VMEM
 f32 = jnp.float32
-
-
-def shifted(value, axis, steps):
-    count = lax.axis_size(axis)
-    leading, last = (max(0, -steps), min(count, count - steps))
-    return lax.ppermute(value, axis, [(source, source + steps) for source in range(leading, last)])
 
 
 def matrices():
@@ -105,9 +99,9 @@
 
 def whole_kernel(
     batches, slots, chunks, mesh_rows, mesh_cols,
-    info, tile, probe_in, pats_in, mats, perm, out_tile, out_probe,
+    spots, tile, probe_in, pats_in, mats, perm, out_tile, out_probe, theirs_info,
     ext, probe, raw, pats, rolled, arrived, grads, gained, acc, base, weight, side, from_left, from_right,
-    above, below, before, psi, pg, got1, half, got2, got3, got4, send, recv, slot_send, slot_recv, local,
+    above, below, before, psi, pg, got1, half, relay, got2, got3, got4, send, recv, slot_send, slot_recv, local,
 ):
     row, col = lax.axis_index("row"), lax.axis_index("col")
     y, x, z, core = lax.div(row, 4), lax.rem(row, 4), lax.div(col, 2), lax.rem(col, 2)
@@ -122,29 +116,47 @@
     down = (lax.rem(row + 1, mesh_rows), col)
     before_me = (row, lax.rem(col + mesh_cols - 1, mesh_cols))
     after_me = (row, lax.rem(col + 1, mesh_cols))
+    down_right = (down[0], after_me[1])
+    up_left = (up[0], before_me[1])
     links = Links(send, recv)
 
     loads = [
         pltpu.make_async_copy(tile.at[:, :, pl.ds(j * SIDE, SIDE)], ext.at[j], local.at[j])
         for j in range(chunks)
     ]
-    loads.append(pltpu.make_async_copy(pats_in, raw, local.at[chunks]))
+    kept = slots - 1
+    for b in range(batches):
+        mine = pl.ds(b * slots, kept)
+        loads.append(pltpu.make_async_copy(pats_in.at[mine], raw.at[mine], local.at[chunks + 2 + b]))
     loads.append(pltpu.make_async_copy(probe_in, probe.at[0], local.at[chunks + 1]))
     for load in loads:
         load.start()
     barrier = pltpu.get_barrier_semaphore()
-    peers = [sibling, up, down, before_me, after_me]
+    peers = [sibling, up, down, before_me, after_me, down_right, up_left]
     peers += [f(j) for f in (along_first, along_second, along_x) for j in (1, 2, 3)]
     for peer in peers:
         pl.semaphore_signal(barrier, inc=1, device_id=peer, device_id_type=MESH)
     pl.semaphore_wait(barrier, len(peers))
 
     rows, cols = iotas()
+    infos = [
+        links.copy(spots, theirs_info.at[i], peer) for i, peer in enumerate((down, after_me, down_right))
+    ]
     rim = links.copy(tile.at[:, :, pl.ds(0, SIDE)], ext.at[chunks], before_me)
-    sent = [rim]
+    handed = [
+        links.copy(pats_in.at[b * slots + kept], raw.at[b * slots + kept], down) for b in range(batches)
+    ]
+    sent = infos + [rim] + handed
+
+    def spot(b, who, s):
+        read = (lambda i: spots[i]) if who == 0 else (lambda i: theirs_info[who - 1, i])
+        r = lax.rem(read(2 * (b * slots + s)), SIDE)
+        c = lax.rem(read(2 * (b * slots + s) + 1), SIDE * chunks)
+        live = (s < read(2 * batches * slots + b)) * 1
+        return lax.div(c, SIDE), r, lax.rem(c, SIDE), live
 
     def where_to(b, who, s, rows_below):
-        k, r, cm, live = [info[b, who, s, j] for j in range(4)]
+        k, r, cm, live = spot(b, who, s)
         inside = (rows < r) if rows_below else (rows >= r)
         return jnp.where(inside & (live == 1), k + (cols < cm).astype(jnp.int32), -1)
 
@@ -155,29 +167,27 @@
             links.copy(ext.at[chunks - 1, :, :, pl.ds(HALF, HALF)], before.at[b], after_me),
         ]
 
-    def slot_copy(b, s, kind):
-        src, dst, peer = (rolled, arrived, up) if kind == 0 else (grads, gained, down)
+    def slot_copy(b, s, kind, away):
+        src, dst = (rolled, arrived) if kind == 0 else (grads, gained)
+        step = (1 - away) * (mesh_rows - 2) if kind == 0 else away * (mesh_rows - 2)
         i = (2 * b + kind) * slots + s
         return pltpu.make_async_remote_copy(
             src_ref=src.at[s],
             dst_ref=dst.at[b, s],
             send_sem=slot_send.at[i],
             recv_sem=slot_recv.at[i],
-            device_id=peer,
+            device_id=(lax.rem(row + 1 + step, mesh_rows), col),
             device_id_type=MESH,
         )
 
-    def start_rims(b):
-        def one(s, carry):
-            k, cm = info[b, 1, s, 0], info[b, 1, s, 2]
-            for part in range(2):
-                rolled[s, part] = jnp.where(cols >= cm, ext[k, part], ext[k + 1, part])
-            slot_copy(b, s, 0).start()
-            return carry
-
-        lax.fori_loop(0, slots, one, 0)
-
-    def order_patterns():
+    def start_rim(b, s):
+        away = int(s == kept)
+        k, r, cm, live = spot(b, 1 - away, s)
+        for part in range(2):
+            rolled[s, part] = jnp.where(cols >= cm, ext[k, part], ext[k + 1, part])
+        slot_copy(b, s, 0, away).start()
+
+    def order_patterns(b):
         def one(i, carry):
             high, low = split(raw[i])
             value = dot(perm[0], high) + dot(perm[0], low)
@@ -185,7 +195,7 @@
             pats[i] = dot(high, perm[1]) + dot(low, perm[1])
             return carry
 
-        lax.fori_loop(0, batches * slots, one, 0)
+        lax.fori_loop(b * slots, (b + 1) * slots, one, 0)
 
     def prepare(b, halos):
         power = probe[b, 0] * probe[b, 0]
@@ -196,7 +206,7 @@
 
         def one(s, carry):
             for who in range(4):
-                value = roll2(pg[2 * MODES], info[b, who, s, 1], info[b, who, s, 2])
+                value = roll2(pg[2 * MODES], *spot(b, who, s)[1:3])
                 chunk = where_to(b, who, s, who % 2 == 1)
                 if who < 2:
                     for j in range(chunks):
@@ -237,14 +247,17 @@
     def run_slots(b):
         pg[...] = jnp.zeros_like(pg)
 
-        def one(s, carry):
-            slot_copy(b, s, 0).wait_recv()
-            k, r, cm, live = [info[b, 0, s, j] for j in range(4)]
+        def one(i, carry):
+            s = lax.rem(2 * i, slots)
+            away = lax.rem(i, 2)
+            slot_copy(b, s, 0, away).wait_recv()
+            k, r, cm, live = [jnp.where(away == 1, t, o) for o, t in zip(spot(b, 0, s), spot(b, 1, s))]
             alive = live.astype(f32)
+            here = (rows - r) * (1 - 2 * away) - away >= 0
             window = []
             for part in range(2):
                 own = jnp.where(cols >= cm, ext[k, part], ext[k + 1, part])
-                value = jnp.where(rows >= r, own, arrived[b, s, part])
+                value = jnp.where(here, own, arrived[b, s, part])
                 window.append(roll2(value, lax.rem(SIDE - r, SIDE), lax.rem(SIDE - cm, SIDE)))
             xr, xi = window
             total_e = total_o = None
@@ -281,17 +294,19 @@
             pg[2 * MODES] += (xr * xr + xi * xi) * alive
             grads[s, 0] = roll2(grad_r, r, cm)
             grads[s, 1] = roll2(grad_i, r, cm)
-            slot_copy(b, s, 1).start()
+            slot_copy(b, s, 1, away).start()
             return carry
 
         lax.fori_loop(0, slots, one, 0)
 
     def gather(b, s):
-        slot_copy(b, s, 1).wait_recv()
+        away = int(s == kept)
+        slot_copy(b, s, 1, away).wait_recv()
         own, theirs = where_to(b, 0, s, False), where_to(b, 1, s, True)
+        mine, others = (gained.at[b, s], grads.at[s]) if away else (grads.at[s], gained.at[b, s])
         for part in range(2):
             for j in range(chunks + 1):
-                value = jnp.where(own == j, grads[s, part], 0.0) + jnp.where(theirs == j, gained[b, s, part], 0.0)
+                value = jnp.where(own == j, mine[part], 0.0) + jnp.where(theirs == j, others[part], 0.0)
                 if s == 0:
                     acc[j, part] = value
                 else:
@@ -308,16 +323,33 @@
         return ones
 
     def reduce_first(ones):
-        twos = []
-        for i, step in enumerate(order):
-            piece = turn(first, step)
+        def piece(i):
             ones[i].wait_recv()
-            mine, there = at(core * HALF, piece, 32), at(0, piece, 32)
-            half[:, there, :] = pg[:, mine, :] + got1[:, there, :]
-            if step:
-                twos.append(links.copy(half.at[:, there, :], got2.at[step - 1], along_first(step)))
-        sent.extend(twos)
-        return twos
+            index = turn(first, order[i])
+            there = at(0, index, 32)
+            half[:, there, :] = pg[:, at(core * HALF, index, 32), :] + got1[:, there, :]
+            return pl.multiple_of(index * 32, 8)
+
+        far = piece(0)
+        rows_of = lambda start, part: pl.ds(pl.multiple_of(start + 16 * part, 8), 16)
+        hops = [links.copy(half.at[:, rows_of(far, p), :], relay.at[p], along_first((1, 3)[p])) for p in range(2)]
+        near, late = [], []
+        for p in range(2):
+            start = piece(1 + p)
+            rows_now = rows_of(start, 1 - p)
+            near.append(
+                links.copy(half.at[:, rows_now, :], got2.at[p, :, pl.ds(16 * (1 - p), 16), :], along_first((1, 3)[p]))
+            )
+            late.append(rows_of(start, p))
+        piece(3)
+        for p in range(2):
+            hops[p].wait_recv()
+            half[:, late[p], :] = half[:, late[p], :] + relay[p]
+            near.append(
+                links.copy(half.at[:, late[p], :], got2.at[p, :, pl.ds(16 * p, 16), :], along_first((1, 3)[p]))
+            )
+        sent.extend(hops + near)
+        return near
 
     def reduce_second(twos):
         threes = []
@@ -326,8 +358,7 @@
         for step in order:
             piece = turn(second, step)
             there, within = at(first * 32, piece, 8), at(0, piece, 8)
-            value = half[:, there, :] + got2[0, :, within, :]
-            half[:, there, :] = value + got2[1, :, within, :] + got2[2, :, within, :]
+            half[:, there, :] = half[:, there, :] + got2[0, :, within, :] + got2[1, :, within, :]
             if step:
                 threes.append(links.copy(half.at[:, there, :], got3.at[step - 1], along_second(step)))
         sent.extend(threes)
@@ -362,41 +393,58 @@
         for copy in copies:
             copy.wait_recv()
         block = probe.at[b + 1, :, at(core * HALF, first, 32), :]
-        twos = [links.copy(block, block, along_first(step)) for step in (2, 1, 3)]
+        twos = [links.copy(block, block, along_first(step)) for step in (1, 3)]
         threes = [links.copy(block, block, sibling)]
         sent.extend(twos + threes)
         return twos, threes
 
     def spread_cores(b, twos, threes):
-        for i, step in ((1, 1), (2, 3), (0, 2)):
-            twos[i].wait_recv()
-            block = probe.at[b + 1, :, at(core * HALF, turn(first, 4 - step), 32), :]
-            copy = links.copy(block, block, sibling)
-            threes.append(copy)
-            sent.append(copy)
+        def to(index, start, count, peer):
+            there = pl.ds(pl.multiple_of(core * HALF + index * 32 + start, 8), count)
+            block = probe.at[b + 1, :, there, :]
+            return links.copy(block, block, peer)
+
+        hops = []
+        for p in range(2):
+            twos[p].wait_recv()
+            index = turn(first, (3, 1)[p])
+            hops.append(to(index, 16 * p, 16, along_first((1, 3)[p])))
+            threes.append(to(index, 0, 32, sibling))
+        for p in range(2):
+            hops[p].wait_recv()
+            threes.append(to(turn(first, 2), 16 * p, 16, sibling))
         for copy in threes:
             copy.wait_recv()
+        sent.extend(hops + threes[1:])
 
     for load in loads[:chunks]:
         load.wait()
     halos = start_halos(0)
     for load in loads[chunks:]:
         load.wait()
-    order_patterns()
+    for copy in infos:
+        copy.wait_recv()
     rim.wait_recv()
-    start_rims(0)
+    start_rim(0, 0)
+    start_rim(0, kept)
     got1s, got2s, got3s, got4s = got1, got2, got3, got4
     stores = []
     for b in range(batches):
         more = b + 1 < batches
         got1, got2, got3, got4 = got1s.at[b], got2s.at[b], got3s.at[b], got4s.at[b]
+        handed[b].wait_recv()
+        order_patterns(b)
         sides = prepare(b, halos)
+        slot_copy(b, 0, 0, 0).wait_send()
+        for s in range(1, kept):
+            start_rim(b, s)
         run_slots(b)
         ones = reduce_cores()
-        for s in range(slots - 1):
+        gather(b, 0)
+        gather(b, kept)
+        twos = reduce_first(ones)
+        for s in range(1, kept):
             gather(b, s)
-        twos = reduce_first(ones)
-        gather(b, slots - 1)
         to_right = links.copy(acc.at[chunks], from_left.at[b], after_me)
         sent.append(to_right)
         if more:
@@ -410,6 +458,8 @@
             copy.wait_send()
         for j in list(range(1, chunks)) + [0]:
             if j == 0:
+                if not more:
+                    twos, threes = spread_first(b, spread)
                 to_right.wait_recv()
             scale = step_object / (weight[j] + object_floor)
             for part in range(2):
@@ -420,8 +470,10 @@
                 store.start()
                 stores.append(store)
         for s in range(slots):
-            slot_copy(b, s, 0).wait_send()
-            slot_copy(b, s, 1).wait_send()
+            away = int(s == kept)
+            if s:
+                slot_copy(b, s, 0, away).wait_send()
+            slot_copy(b, s, 1, away).wait_send()
         if more:
             to_left.wait_recv()
             for copy in sides:
@@ -429,10 +481,11 @@
             scale = step_object / (side[2] + object_floor)
             for part in range(2):
                 ext[chunks, part] = side[part] - scale * (acc[chunks, part] + from_right[part])
-            start_rims(b + 1)
+            start_rim(b + 1, 0)
+            start_rim(b + 1, kept)
             halos = start_halos(b + 1)
             spread = spread_second(b, fours)
-        twos, threes = spread_first(b, spread)
+            twos, threes = spread_first(b, spread)
         spread_cores(b, twos, threes)
         if more:
             for copy in sent:
@@ -451,13 +504,8 @@
     chunks = tile_cols // SIDE
     batches, slots = offsets.shape[:2]
     mesh_rows, mesh_cols = lax.axis_size("row"), lax.axis_size("col")
-    anchor = jnp.stack([lax.axis_index("row") * tile_rows, lax.axis_index("col") * tile_cols])
-    local = offsets - anchor[None, None, :]
-    row_at, col_at = local[..., 0], local[..., 1]
-    live = (jnp.arange(slots)[None, :] < live_counts).astype(jnp.int32)
-    own = jnp.stack([col_at // SIDE, row_at, col_at % SIDE, live], axis=-1)
-    two = jnp.stack([own, shifted(own, "row", 1)], axis=1)
-    info = jnp.concatenate([two, shifted(two, "col", 1)], axis=1)
+    spots = jnp.concatenate([offsets.reshape(-1), live_counts.reshape(-1)])
+    spots = jnp.pad(spots, (0, 128 - spots.shape[0]))
     perm = np.zeros((SIDE, SIDE), np.float32)
     j = np.arange(SIDE)
     perm[j, (j % 2) * HALF + j // 2] = 1.0
@@ -476,6 +524,7 @@
             jax.ShapeDtypeStruct((2 * MODES, SIDE, SIDE), f32),
         ],
         scratch_shapes=[
+            pltpu.SMEM((3, 128), jnp.int32),
             buf(chunks + 1, *block),
             buf(batches + 1, 2 * MODES, SIDE, SIDE),
             buf(batches * slots, SIDE, SIDE),
@@ -497,21 +546,22 @@
             buf(PLANES, SIDE, SIDE),
             buf(batches, PLANES, HALF, SIDE),
             buf(PLANES, HALF, SIDE),
-            buf(batches, 3, PLANES, 32, SIDE),
+            buf(2, PLANES, 16, SIDE),
+            buf(batches, 2, PLANES, 32, SIDE),
             buf(batches, 3, PLANES, 8, SIDE),
             buf(batches, 4, PLANES, 8, SIDE),
-            dma((80,)),
-            dma((80,)),
+            dma((100,)),
+            dma((100,)),
             dma((2 * batches * slots,)),
             dma((2 * batches * slots,)),
-            dma((chunks + 2,)),
+            dma((chunks + 2 + batches,)),
         ],
         compiler_params=pltpu.CompilerParams(
             collective_id=0, has_side_effects=True, vmem_limit_bytes=60 * 2**20
         ),
         name="reconstruct",
     )(
-        info,
+        spots,
         object_field,
         probe_modes.reshape(2 * MODES, SIDE, SIDE),
         patterns.reshape(batches * slots, SIDE, SIDE),

time: 236 us -> 180 us (0.76)
  Pallas kernels: 215 us -> 170 us
  starting transfers between devices: 8.89 us -> 0 us
    pallas_call x1, Pallas kernels: 215 us -> 170 us  [shards(): pl.pallas_call(functools.partial(whole_kernel, batches, slots, chunks, me...]
    ppermute x2 -> x0, starting transfers between devices: 8.89 us -> none  [shifted(): lax.ppermute(value, axis, [(source, source + steps) for source in range(l...]
    unnamed x4 -> x5, local copies, waits for them, and re-layouts: 4.63 us -> 5.4 us
  transfers between devices with their start and end apart: 2 -> 0, of which waited for: 2 -> 0; matrix products, arithmetic and copies ran while one was open for 0% -> 0% of each run, Pallas kernels for 0% -> 0%
where the time goes in v4:
time: 180 us; the launch traced here: 178 us
  Pallas kernels  170 us (94%)
  local copies, waits for them, and re-layouts  6.01 us (3%)
    pallas_call x1, Pallas kernels, shards(): pl.pallas_call(functools.partial(whole_kernel, batches, slots, chunks, me...  170 us
    unnamed x5, local copies, waits for them, and re-layouts  5.4 us

profile of v4, /device:TPU:1, one launch (start us, length us, event | category | flops | bytes accessed | tf_op | source)
XLA Modules:
  0.0 177.8 jit_solution(10550373004984353763)
XLA Ops:
  0.6 0.8 copy.10
  1.4 0.1 reshape.19
  1.5 0.7 pad_add_fusion
  2.2 0.5 pad.4.spots
  2.7 170.4 %reconstruct.1 = (f32[2,256,1024]{2,1,0:T(8,128)}, f32[8,256,256]{2,1,0:T(8,128)}) custom-call(s32[128]{0:T(128)} %pad.4.spots, f32[2,256,1024]{2,1,0:T(8,128)} %tile.1, f32[8,256,256]{2,1,0:T(8,128)} %bitcast.4, f32[6,256,256]{2,1,0:T(8,128)} %bitcast.6, bf16[8,256,256]{2,1,0:T(8,128)(2,1)} %constant.7.clone.mats, bf16[2,256,256]{2,1,0:T(8,128)(2,1)} %constant.6.clone.perm), custom_call_target="tpu_custom_call" | custom-call | tf_op jit(solution)/shard_map/reconstruct/pallas_call | solution.py:518
  173.2 0.0 copy-start
  173.2 3.3 %copy.13 = f32[2,256,1024]{2,1,0:T(8,128)} copy(f32[2,256,1024]{2,1,0:T(8,128)} %get-tuple-element.8) | data formatting | bytes 4194304
  176.5 0.0 copy-done
  176.5 1.3 copy.14
Async XLA Ops:
  173.2 3.3 %copy-start = (f32[8,256,256]{2,1,0:T(8,128)S(1)}, f32[8,256,256]{2,1,0:T(8,128)}, u32[]{:S(2)}) copy-start(f32[8,256,256]{2,1,0:T(8,128)} %get-tuple-element.5) | copy-start | bytes 6291460

commit v5 on v4

--- a/solution.py
+++ b/solution.py
@@ -48,7 +48,8 @@
 def left(mats, index, value):
     high, low = split(value)
     a, b = mats[index], mats[index + 1]
-    return dot(a, high) + dot(b, high) + dot(a, low)
+    both = dot(cat(0, a, b), high)
+    return both[:SIDE] + both[SIDE:] + dot(a, low)
 
 
 def right(value, mats, index):
@@ -100,8 +101,8 @@
 def whole_kernel(
     batches, slots, chunks, mesh_rows, mesh_cols,
     spots, tile, probe_in, pats_in, mats, perm, out_tile, out_probe, theirs_info,
-    ext, probe, raw, pats, rolled, arrived, grads, gained, acc, base, weight, side, from_left, from_right,
-    above, below, before, psi, pg, got1, half, relay, got2, got3, got4, send, recv, slot_send, slot_recv, local,
+    ext, rim_in, probe, raw, pats, rolled, arrived, grads, gained, acc, base, weight, side, from_left, from_right,
+    above, below, before, psi, middle, window, total, pg, got1, half, got2, got3, got4, send, recv, slot_send, slot_recv, local,
 ):
     row, col = lax.axis_index("row"), lax.axis_index("col")
     y, x, z, core = lax.div(row, 4), lax.rem(row, 4), lax.div(col, 2), lax.rem(col, 2)
@@ -142,11 +143,14 @@
     infos = [
         links.copy(spots, theirs_info.at[i], peer) for i, peer in enumerate((down, after_me, down_right))
     ]
-    rim = links.copy(tile.at[:, :, pl.ds(0, SIDE)], ext.at[chunks], before_me)
-    handed = [
-        links.copy(pats_in.at[b * slots + kept], raw.at[b * slots + kept], down) for b in range(batches)
-    ]
-    sent = infos + [rim] + handed
+    parts = [pl.ds(0, HALF), pl.ds(HALF, HALF)]
+    rims = [links.copy(tile.at[:, p, pl.ds(0, SIDE)], rim_in.at[:, p, :], before_me) for p in parts]
+
+    def hand(b):
+        return links.copy(pats_in.at[b * slots + kept], raw.at[b * slots + kept], down)
+
+    handed = [hand(0)]
+    sent = infos + rims
 
     def spot(b, who, s):
         read = (lambda i: spots[i]) if who == 0 else (lambda i: theirs_info[who - 1, i])
@@ -167,25 +171,32 @@
             links.copy(ext.at[chunks - 1, :, :, pl.ds(HALF, HALF)], before.at[b], after_me),
         ]
 
-    def slot_copy(b, s, kind, away):
+    def slot_copy(b, s, kind, away, there=None):
         src, dst = (rolled, arrived) if kind == 0 else (grads, gained)
         step = (1 - away) * (mesh_rows - 2) if kind == 0 else away * (mesh_rows - 2)
         i = (2 * b + kind) * slots + s
         return pltpu.make_async_remote_copy(
-            src_ref=src.at[s],
-            dst_ref=dst.at[b, s],
+            src_ref=src.at[s] if there is None else src.at[s, :, there, :],
+            dst_ref=dst.at[b, s] if there is None else dst.at[b, s, :, there, :],
             send_sem=slot_send.at[i],
             recv_sem=slot_recv.at[i],
             device_id=(lax.rem(row + 1 + step, mesh_rows), col),
             device_id_type=MESH,
         )
 
-    def start_rim(b, s):
+    def start_rim(b, s, part=None):
         away = int(s == kept)
         k, r, cm, live = spot(b, 1 - away, s)
-        for part in range(2):
-            rolled[s, part] = jnp.where(cols >= cm, ext[k, part], ext[k + 1, part])
-        slot_copy(b, s, 0, away).start()
+        there = pl.ds(0, SIDE) if part is None else parts[part]
+        right_of = (cols if part is None else cols[:HALF]) >= cm
+        for plane in range(2):
+            if part is None:
+                after = ext[k + 1, plane, there]
+            else:
+                inside = ext[jnp.minimum(k + 1, chunks - 1), plane, there]
+                after = jnp.where(k == chunks - 1, rim_in[plane, there], inside)
+            rolled[s, plane, there] = jnp.where(right_of, ext[k, plane, there], after)
+        slot_copy(b, s, 0, away, there).start()
 
     def order_patterns(b):
         def one(i, carry):
@@ -197,16 +208,16 @@
 
         lax.fori_loop(b * slots, (b + 1) * slots, one, 0)
 
-    def prepare(b, halos):
+    def weigh(b):
         power = probe[b, 0] * probe[b, 0]
         for plane in range(1, 2 * MODES):
             power = power + probe[b, plane] * probe[b, plane]
-        pg[2 * MODES] = power
+        window[0] = power
         weight[...] = jnp.zeros_like(weight)
 
         def one(s, carry):
             for who in range(4):
-                value = roll2(pg[2 * MODES], *spot(b, who, s)[1:3])
+                value = roll2(window[0], *spot(b, who, s)[1:3])
                 chunk = where_to(b, who, s, who % 2 == 1)
                 if who < 2:
                     for j in range(chunks):
@@ -216,6 +227,8 @@
             return carry
 
         lax.fori_loop(0, slots, one, 0)
+
+    def smooth(b, halos):
         for copy in halos:
             copy.wait_recv()
         for part in range(2):
@@ -235,14 +248,6 @@
                 neighbours += jnp.where(cols == 0, lhs, pltpu.roll(here, 1, 1))
                 neighbours += jnp.where(cols == SIDE - 1, rhs, pltpu.roll(here, SIDE - 1, 1))
                 base[j, part] = here + (step_object * smoothing) * (neighbours - 4.0 * here)
-        if b + 1 < batches:
-            copies = [
-                links.copy(base.at[0], side.at[pl.ds(0, 2)], before_me),
-                links.copy(weight.at[0], side.at[2], before_me),
-            ]
-            sent.extend(copies)
-            return copies
-        return []
 
     def run_slots(b):
         pg[...] = jnp.zeros_like(pg)
@@ -254,46 +259,72 @@
             k, r, cm, live = [jnp.where(away == 1, t, o) for o, t in zip(spot(b, 0, s), spot(b, 1, s))]
             alive = live.astype(f32)
             here = (rows - r) * (1 - 2 * away) - away >= 0
-            window = []
             for part in range(2):
                 own = jnp.where(cols >= cm, ext[k, part], ext[k + 1, part])
                 value = jnp.where(here, own, arrived[b, s, part])
-                window.append(roll2(value, lax.rem(SIDE - r, SIDE), lax.rem(SIDE - cm, SIDE)))
-            xr, xi = window
-            total_e = total_o = None
-            for m in range(MODES):
-                pr, pi = probe[b, 2 * m], probe[b, 2 * m + 1]
+                window[part] = roll2(value, lax.rem(SIDE - r, SIDE), lax.rem(SIDE - cm, SIDE))
+
+            def rows_in(m):
+                pr, pi, xr, xi = probe[b, 2 * m], probe[b, 2 * m + 1], window[0], window[1]
                 wr, wi = pr * xr - pi * xi, pr * xi + pi * xr
-                even = left(mats, 0, cat(0, wr[:HALF] + wr[HALF:], wi[:HALF] + wi[HALF:]))
-                odd = left(mats, 4, cat(0, wr[:HALF] - wr[HALF:], wi[:HALF] - wi[HALF:]))
-                tr, ti = cat(0, even[:HALF], odd[:HALF]), cat(0, even[HALF:], odd[HALF:])
-                pe = right(cat(1, tr[:, :HALF] + tr[:, HALF:], ti[:, :HALF] + ti[:, HALF:]), mats, 2)
-                po = right(cat(1, tr[:, :HALF] - tr[:, HALF:], ti[:, :HALF] - ti[:, HALF:]), mats, 6)
-                psi[m, 0], psi[m, 1] = pe, po
-                total_e = pe * pe if m == 0 else total_e + pe * pe
-                total_o = po * po if m == 0 else total_o + po * po
-            pattern = pats[b * slots + s]
-            de = (total_e[:, :HALF] + total_e[:, HALF:] - pattern[:, :HALF]) * alive
-            do = (total_o[:, :HALF] + total_o[:, HALF:] - pattern[:, HALF:]) * alive
-            de, do = cat(1, de, de), cat(1, do, do)
-            grad_r = grad_i = None
-            for m in range(MODES):
-                ue, uo = right(psi[m, 0] * de, mats, 0), right(psi[m, 1] * do, mats, 4)
-                plus, minus = ue + uo, ue - uo
-                tr, ti = cat(1, plus[:, :HALF], minus[:, :HALF]), cat(1, plus[:, HALF:], minus[:, HALF:])
-                ze = left(mats, 2, cat(0, tr[:HALF], ti[:HALF]))
-                zo = left(mats, 6, cat(0, tr[HALF:], ti[HALF:]))
+                middle[m, 0] = left(mats, 0, cat(0, wr[:HALF] + wr[HALF:], wi[:HALF] + wi[HALF:]))
+                middle[m, 1] = left(mats, 4, cat(0, wr[:HALF] - wr[HALF:], wi[:HALF] - wi[HALF:]))
+
+            def cols_in(pair):
+                sums, diffs = [], []
+                for m in pair:
+                    for q in range(2):
+                        value = middle[m, q]
+                        tr, ti = value[:HALF], value[HALF:]
+                        sums.append(cat(1, tr[:, :HALF] + tr[:, HALF:], ti[:, :HALF] + ti[:, HALF:]))
+                        diffs.append(cat(1, tr[:, :HALF] - tr[:, HALF:], ti[:, :HALF] - ti[:, HALF:]))
+                for q, (values, index) in enumerate(((sums, 2), (diffs, 6))):
+                    far = right(cat(0, *values), mats, index)
+                    for j, m in enumerate(pair):
+                        value = far[j * SIDE : (j + 1) * SIDE]
+                        psi[m, q] = value
+                        total[q] = value * value if m == 0 else total[q] + value * value
+
+            def cols_out(pair):
+                ue = right(cat(0, *[psi[m, 0] * total[0] for m in pair]), mats, 0)
+                uo = right(cat(0, *[psi[m, 1] * total[1] for m in pair]), mats, 4)
+                for j, m in enumerate(pair):
+                    e, o = ue[j * SIDE : (j + 1) * SIDE], uo[j * SIDE : (j + 1) * SIDE]
+                    plus, minus = e + o, e - o
+                    tr, ti = cat(1, plus[:, :HALF], minus[:, :HALF]), cat(1, plus[:, HALF:], minus[:, HALF:])
+                    middle[m, 0], middle[m, 1] = cat(0, tr[:HALF], ti[:HALF]), cat(0, tr[HALF:], ti[HALF:])
+
+            def rows_out(m):
+                ze, zo = left(mats, 2, middle[m, 0]), left(mats, 6, middle[m, 1])
                 plus, minus = ze + zo, ze - zo
                 br, bi = cat(0, plus[:HALF], minus[:HALF]), cat(0, plus[HALF:], minus[HALF:])
-                pr, pi = probe[b, 2 * m], probe[b, 2 * m + 1]
+                pr, pi, xr, xi = probe[b, 2 * m], probe[b, 2 * m + 1], window[0], window[1]
                 gr, gi = pr * br + pi * bi, pr * bi - pi * br
-                grad_r = gr if m == 0 else grad_r + gr
-                grad_i = gi if m == 0 else grad_i + gi
-                pg[2 * m] += xr * br + xi * bi
-                pg[2 * m + 1] += xr * bi - xi * br
-            pg[2 * MODES] += (xr * xr + xi * xi) * alive
-            grads[s, 0] = roll2(grad_r, r, cm)
-            grads[s, 1] = roll2(grad_i, r, cm)
+                grads[s, 0] = gr if m == 0 else grads[s, 0] + gr
+                grads[s, 1] = gi if m == 0 else grads[s, 1] + gi
+                pg[1 + 2 * m] += xr * br + xi * bi
+                pg[2 + 2 * m] += xr * bi - xi * br
+
+            pairs = [tuple(range(m, m + 2)) for m in range(0, MODES, 2)]
+            for m in pairs[0]:
+                rows_in(m)
+            for p, pair in enumerate(pairs):
+                for m in pairs[p + 1] if p + 1 < len(pairs) else ():
+                    rows_in(m)
+                cols_in(pair)
+            for q in range(2):
+                value = total[q]
+                value = value[:, :HALF] + value[:, HALF:] - pats[b * slots + s, :, pl.ds(q * HALF, HALF)]
+                total[q] = cat(1, value, value) * alive
+            cols_out(pairs[0])
+            for p, pair in enumerate(pairs):
+                if p + 1 < len(pairs):
+                    cols_out(pairs[p + 1])
+                for m in pair:
+                    rows_out(m)
+            pg[0] += (window[0] * window[0] + window[1] * window[1]) * alive
+            for part in range(2):
+                grads[s, part] = roll2(grads[s, part], r, cm)
             slot_copy(b, s, 1, away).start()
             return carry
 
@@ -312,110 +343,79 @@
                 else:
                     acc[j, part] += value
 
-    order = (2, 1, 3, 0)
-
-    def reduce_cores():
-        ones = []
-        for step in order:
-            theirs, there = at((1 - core) * HALF, turn(second, step), 32), at(0, turn(second, step), 32)
-            ones.append(links.copy(pg.at[:, theirs, :], got1.at[:, there, :], sibling))
-        sent.extend(ones)
-        return ones
-
-    def reduce_first(ones):
-        def piece(i):
-            ones[i].wait_recv()
-            index = turn(first, order[i])
-            there = at(0, index, 32)
-            half[:, there, :] = pg[:, at(core * HALF, index, 32), :] + got1[:, there, :]
-            return pl.multiple_of(index * 32, 8)
-
-        far = piece(0)
-        rows_of = lambda start, part: pl.ds(pl.multiple_of(start + 16 * part, 8), 16)
-        hops = [links.copy(half.at[:, rows_of(far, p), :], relay.at[p], along_first((1, 3)[p])) for p in range(2)]
-        near, late = [], []
-        for p in range(2):
-            start = piece(1 + p)
-            rows_now = rows_of(start, 1 - p)
-            near.append(
-                links.copy(half.at[:, rows_now, :], got2.at[p, :, pl.ds(16 * (1 - p), 16), :], along_first((1, 3)[p]))
-            )
-            late.append(rows_of(start, p))
-        piece(3)
-        for p in range(2):
-            hops[p].wait_recv()
-            half[:, late[p], :] = half[:, late[p], :] + relay[p]
-            near.append(
-                links.copy(half.at[:, late[p], :], got2.at[p, :, pl.ds(16 * p, 16), :], along_first((1, 3)[p]))
-            )
-        sent.extend(hops + near)
-        return near
-
-    def reduce_second(twos):
-        threes = []
+    groups = [pl.ds(0, 1 + MODES), pl.ds(1 + MODES, MODES)]
+
+    def reduce_cores(g):
+        theirs = at((1 - core) * HALF, 0, HALF)
+        one = links.copy(pg.at[groups[g], theirs, :], got1.at[groups[g]], sibling)
+        sent.append(one)
+        return [one]
+
+    def reduce_first(g, ones):
+        twos = []
+        for copy in ones:
+            copy.wait_recv()
+        for step in (2, 1, 3, 0):
+            piece = turn(first, step)
+            mine, there = at(core * HALF, piece, 32), at(0, piece, 32)
+            half[groups[g], there, :] = pg[groups[g], mine, :] + got1[groups[g], there, :]
+            if step:
+                src, dst = half.at[groups[g], there, :], got2.at[step - 1, groups[g]]
+                twos.append(links.copy(src, dst, along_first(step)))
+        sent.extend(twos)
+        return twos
+
+    def reduce_second(g, twos):
+        threes, planes = [], groups[g]
         for copy in twos:
             copy.wait_recv()
-        for step in order:
+        for step in (2, 1, 3, 0):
             piece = turn(second, step)
             there, within = at(first * 32, piece, 8), at(0, piece, 8)
-            half[:, there, :] = half[:, there, :] + got2[0, :, within, :] + got2[1, :, within, :]
+            value = half[planes, there, :] + got2[0, planes, within, :]
+            half[planes, there, :] = value + got2[1, planes, within, :] + got2[2, planes, within, :]
             if step:
-                threes.append(links.copy(half.at[:, there, :], got3.at[step - 1], along_second(step)))
+                src, dst = half.at[planes, there, :], got3.at[step - 1, planes]
+                threes.append(links.copy(src, dst, along_second(step)))
         sent.extend(threes)
         return threes
 
-    def reduce_x(threes):
-        fours = []
+    def reduce_x(g, threes):
+        fours, planes = [], groups[g]
         for copy in threes:
             copy.wait_recv()
         there = at(first * 32, second, 8)
-        got4[x] = half[:, there, :] + got3[0] + got3[1] + got3[2]
+        got4[x, planes] = half[planes, there, :] + got3[0, planes] + got3[1, planes] + got3[2, planes]
         for step in (2, 1, 3):
-            fours.append(links.copy(got4.at[x], got4.at[x], along_x(step)))
+            fours.append(links.copy(got4.at[x, planes], got4.at[x, planes], along_x(step)))
         sent.extend(fours)
         return fours
 
-    def spread_second(b, fours):
+    def spread(b, g, block, peers):
+        planes = probe.at[b + 1, pl.ds(g * MODES, MODES)]
+        copies = [links.copy(planes.at[:, block, :], planes.at[:, block, :], peer) for peer in peers]
+        sent.extend(copies)
+        return copies
+
+    def spread_second(b, g, fours):
         for copy in fours:
             copy.wait_recv()
-        total = got4[0] + got4[1] + got4[2] + got4[3]
-        scale = step_probe / (total[2 * MODES] + probe_floor)
         mine = at(core * HALF + first * 32, second, 8)
-        new = probe.at[b + 1]
-        for plane in range(2 * MODES):
-            new[plane, mine, :] = probe[b, plane, mine, :] - scale * total[plane]
-        block = new.at[:, mine, :]
-        copies = [links.copy(block, block, along_second(step)) for step in (2, 1, 3)]
-        sent.extend(copies)
-        return copies
-
-    def spread_first(b, copies):
+        scale = step_probe / (got4[0, 0] + got4[1, 0] + got4[2, 0] + got4[3, 0] + probe_floor)
+        for plane in range(g * MODES, (g + 1) * MODES):
+            grad = got4[0, plane + 1] + got4[1, plane + 1] + got4[2, plane + 1] + got4[3, plane + 1]
+            probe[b + 1, plane, mine, :] = probe[b, plane, mine, :] - scale * grad
+        return spread(b, g, mine, [along_second(step) for step in (2, 1, 3)])
+
+    def spread_first(b, g, copies):
         for copy in copies:
             copy.wait_recv()
-        block = probe.at[b + 1, :, at(core * HALF, first, 32), :]
-        twos = [links.copy(block, block, along_first(step)) for step in (1, 3)]
-        threes = [links.copy(block, block, sibling)]
-        sent.extend(twos + threes)
-        return twos, threes
-
-    def spread_cores(b, twos, threes):
-        def to(index, start, count, peer):
-            there = pl.ds(pl.multiple_of(core * HALF + index * 32 + start, 8), count)
-            block = probe.at[b + 1, :, there, :]
-            return links.copy(block, block, peer)
-
-        hops = []
-        for p in range(2):
-            twos[p].wait_recv()
-            index = turn(first, (3, 1)[p])
-            hops.append(to(index, 16 * p, 16, along_first((1, 3)[p])))
-            threes.append(to(index, 0, 32, sibling))
-        for p in range(2):
-            hops[p].wait_recv()
-            threes.append(to(turn(first, 2), 16 * p, 16, sibling))
-        for copy in threes:
+        return spread(b, g, at(core * HALF, first, 32), [along_first(step) for step in (2, 1, 3)])
+
+    def spread_cores(b, g, copies):
+        for copy in copies:
             copy.wait_recv()
-        sent.extend(hops + threes[1:])
+        return spread(b, g, at(core * HALF, 0, HALF), [sibling])
 
     for load in loads[:chunks]:
         load.wait()
@@ -424,25 +424,41 @@
         load.wait()
     for copy in infos:
         copy.wait_recv()
-    rim.wait_recv()
-    start_rim(0, 0)
+    for part in range(2):
+        rims[part].wait_recv()
+        start_rim(0, 0, part)
+    ext[chunks] = rim_in[...]
     start_rim(0, kept)
+    handed += [hand(b) for b in range(1, batches)]
+    sent += handed
+    both = range(2)
     got1s, got2s, got3s, got4s = got1, got2, got3, got4
     stores = []
     for b in range(batches):
         more = b + 1 < batches
         got1, got2, got3, got4 = got1s.at[b], got2s.at[b], got3s.at[b], got4s.at[b]
-        handed[b].wait_recv()
-        order_patterns(b)
-        sides = prepare(b, halos)
-        slot_copy(b, 0, 0, 0).wait_send()
-        for s in range(1, kept):
-            start_rim(b, s)
+        if b == 0:
+            handed[0].wait_recv()
+            order_patterns(0)
+            smooth(0, halos)
+        if more:
+            weigh(b)
+            sides = [
+                links.copy(base.at[0], side.at[pl.ds(0, 2)], before_me),
+                links.copy(weight.at[0], side.at[2], before_me),
+            ]
+        if b == 0:
+            slot_copy(b, 0, 0, 0).wait_send()
+            for s in range(1, kept):
+                start_rim(b, s)
         run_slots(b)
-        ones = reduce_cores()
+        ones = [reduce_cores(g) for g in both]
+        twos = [reduce_first(g, ones[g]) for g in both]
         gather(b, 0)
+        if not more:
+            weigh(b)
         gather(b, kept)
-        twos = reduce_first(ones)
+        threes = [reduce_second(g, twos[g]) for g in both]
         for s in range(1, kept):
             gather(b, s)
         to_right = links.copy(acc.at[chunks], from_left.at[b], after_me)
@@ -450,16 +466,12 @@
         if more:
             to_left = links.copy(acc.at[0], from_right, before_me)
             sent.append(to_left)
-        threes = reduce_second(twos)
-        fours = reduce_x(threes)
-        if not more:
-            spread = spread_second(b, fours)
+        fours = [reduce_x(g, threes[g]) for g in both]
         for copy in halos:
             copy.wait_send()
         for j in list(range(1, chunks)) + [0]:
             if j == 0:
-                if not more:
-                    twos, threes = spread_first(b, spread)
+                fives = [spread_second(b, g, fours[g]) for g in both]
                 to_right.wait_recv()
             scale = step_object / (weight[j] + object_floor)
             for part in range(2):
@@ -484,9 +496,21 @@
             start_rim(b + 1, 0)
             start_rim(b + 1, kept)
             halos = start_halos(b + 1)
-            spread = spread_second(b, fours)
-            twos, threes = spread_first(b, spread)
-        spread_cores(b, twos, threes)
+        sixes = [spread_first(b, g, fives[g]) for g in both]
+        if more:
+            for copy in sides:
+                copy.wait_send()
+            handed[b + 1].wait_recv()
+            order_patterns(b + 1)
+            smooth(b + 1, halos)
+        sevens = [spread_cores(b, g, sixes[g]) for g in both]
+        if more:
+            slot_copy(b + 1, 0, 0, 0).wait_send()
+            for s in range(1, kept):
+                start_rim(b + 1, s)
+        for copies in sevens:
+            for copy in copies:
+                copy.wait_recv()
         if more:
             for copy in sent:
                 copy.wait_send()
@@ -526,6 +550,7 @@
         scratch_shapes=[
             pltpu.SMEM((3, 128), jnp.int32),
             buf(chunks + 1, *block),
+            buf(*block),
             buf(batches + 1, 2 * MODES, SIDE, SIDE),
             buf(batches * slots, SIDE, SIDE),
             buf(batches * slots, SIDE, SIDE),
@@ -543,15 +568,17 @@
             buf(batches, chunks, 2, 8, SIDE),
             buf(batches, 2, SIDE, HALF),
             buf(MODES, *block),
+            buf(MODES, *block),
+            buf(*block),
+            buf(*block),
             buf(PLANES, SIDE, SIDE),
             buf(batches, PLANES, HALF, SIDE),
             buf(PLANES, HALF, SIDE),
-            buf(2, PLANES, 16, SIDE),
-            buf(batches, 2, PLANES, 32, SIDE),
+            buf(batches, 3, PLANES, 32, SIDE),
             buf(batches, 3, PLANES, 8, SIDE),
             buf(batches, 4, PLANES, 8, SIDE),
-            dma((100,)),
-            dma((100,)),
+            dma((110,)),
+            dma((110,)),
             dma((2 * batches * slots,)),
             dma((2 * batches * slots,)),
             dma((chunks + 2 + batches,)),

time: 180 us -> 181 us (level); the launches traced: 178 us -> 181 us
  Pallas kernels: 170 us -> 173 us
    pallas_call x1, Pallas kernels: 170 us -> 173 us  [shards(): pl.pallas_call(functools.partial(whole_kernel, batches, slots, chunks, me...]
where the time goes in v5:
time: 181 us
  Pallas kernels  173 us (96%)
  local copies, waits for them, and re-layouts  6.01 us (3%)
    pallas_call x1, Pallas kernels, shards(): pl.pallas_call(functools.partial(whole_kernel, batches, slots, chunks, me...  173 us
    unnamed x5, local copies, waits for them, and re-layouts  5.4 us

profile of v5, /device:TPU:1, one launch (start us, length us, event | category | flops | bytes accessed | tf_op | source)
XLA Modules:
  0.0 180.8 jit_solution(12996110676118047934)
XLA Ops:
  0.6 0.8 copy.10
  1.4 0.1 reshape.19
  1.5 0.7 pad_add_fusion
  2.2 0.5 pad.4.spots
  2.7 173.4 %reconstruct.1 = (f32[2,256,1024]{2,1,0:T(8,128)}, f32[8,256,256]{2,1,0:T(8,128)}) custom-call(s32[128]{0:T(128)} %pad.4.spots, f32[2,256,1024]{2,1,0:T(8,128)} %tile.1, f32[8,256,256]{2,1,0:T(8,128)} %bitcast.4, f32[6,256,256]{2,1,0:T(8,128)} %bitcast.6, bf16[8,256,256]{2,1,0:T(8,128)(2,1)} %constant.7.clone.mats, bf16[2,256,256]{2,1,0:T(8,128)(2,1)} %constant.6.clone.perm), custom_call_target="tpu_custom_call" | custom-call | tf_op jit(solution)/shard_map/reconstruct/pallas_call | solution.py:542
  176.1 0.0 copy-start
  176.1 3.3 %copy.13 = f32[2,256,1024]{2,1,0:T(8,128)} copy(f32[2,256,1024]{2,1,0:T(8,128)} %get-tuple-element.8) | data formatting | bytes 4194304
  179.4 0.0 copy-done
  179.5 1.3 copy.14
Async XLA Ops:
  176.1 3.3 %copy-start = (f32[8,256,256]{2,1,0:T(8,128)S(1)}, f32[8,256,256]{2,1,0:T(8,128)}, u32[]{:S(2)}) copy-start(f32[8,256,256]{2,1,0:T(8,128)} %get-tuple-element.5) | copy-start | bytes 6291460
